TPU v7x, 256 devices: a whole 4x4x8 slice. The times are simulated.
256 devices in a mesh: half: 2 (over core), cls: 32 (over y, z), tile: 4 (over x).
Axes of the slice: x: 4, y: 4, z: 8, core: 2. Of those that a mesh axis runs over, the one named last changes fastest.
Arguments:
- images: bfloat16 [8192, 256, 256], P(('half', 'cls', 'tile')), may hold values from -32 to 32
- references: bfloat16 [2, 64, 256, 256], P('half', 'cls'), may hold values from -16 to 16
- image_owner: int32 [8192, 1], P(('half', 'cls', 'tile')), may hold values from 0 to 31; in each aligned block of 32 rows (0 to 31, 32 to 63, ...) at most 2 rows name the same one
- image_class: int32 [8192], P(('half', 'cls', 'tile')), may hold values from 0 to 1
- defocus_bin: int32 [8192], P(('half', 'cls', 'tile')), may hold values from 0 to 15
- slice_cells: int32 [64, 128], replicated, may hold values from 0 to 16383, as said below
Outputs:
- half_maps: float32 [2, 16384, 256], P('half', ('cls', 'tile'))
Inputs may be any that keep to these rules, and one draw needn't show every extreme that they name: `image_owner`: among the 32 images of one device no owner is named more than 2 times, and in every draw some device names some owner exactly 2 times. `slice_cells`: take the 256 entries of the classes of one owner (rows o * 2 to o * 2 + 1) and the blocks of 128 consecutive cells: no block holds more than 4 of these entries, and for every owner some block holds exactly 4.
All inputs are finite; a program needn't handle non-finite values.
Results may differ from a plain program's by a relative error of at most 0.008.
Values may be sent and summed in bfloat16 or wider, within the bound.
A program may use at most 128 MiB of HBM per device.

v0:
```python
import math

import jax
import jax.numpy as jnp
from jax import lax
from jax.sharding import PartitionSpec as P

PIX = 256
KF = 128
CLS_DEV = 2
BINS = 16
SHELLS = 64


sharpness = 40.0
ctf_scale = 6.0
amp_phase = 0.1


def swapped(block, axis, bit):
    count = lax.axis_size(axis)
    route = []
    for low in range(count):
        high = low | 1 << bit
        if high != low and high < count:
            route += [(low, high), (high, low)]
    return lax.ppermute(block, axis, route)


def dft_tables():
    sample_pos = jnp.arange(PIX, dtype=jnp.int32)[:, None]
    freq_pos = jnp.arange(KF, dtype=jnp.int32)[None, :] - KF // 2
    angles = (sample_pos * freq_pos % PIX).astype(jnp.float32) * (2.0 * math.pi / PIX)
    scaling = 1.0 / math.sqrt(PIX)
    return (
        (jnp.cos(angles) * scaling).astype(jnp.bfloat16),
        (jnp.sin(angles) * scaling).astype(jnp.bfloat16),
    )


def forward(planes, cos_table, sin_table):
    number = planes.shape[0]
    section_one = jnp.dot(
        planes.reshape(number * PIX, PIX),
        jnp.concatenate([cos_table, sin_table], 1),
        preferred_element_type=jnp.float32,
    )
    section_one = section_one.astype(jnp.bfloat16).reshape(number, PIX, 2 * KF)
    stacked = jnp.concatenate([cos_table.T, sin_table.T], 0)
    section_two = jnp.einsum(
        "kp,npq->nkq", stacked, section_one, preferred_element_type=jnp.float32
    )
    cos_p = section_two[:, :KF, :KF]
    cos_q = section_two[:, :KF, KF:]
    sin_p = section_two[:, KF:, :KF]
    sin_q = section_two[:, KF:, KF:]
    return jnp.concatenate([cos_p - sin_q, -(sin_p + cos_q)], 2)


def inverse(spectra, cos_table, sin_table):
    number = spectra.shape[0]
    upper = jnp.concatenate([cos_table.T, sin_table.T], 1)
    lower = jnp.concatenate([-sin_table.T, cos_table.T], 1)
    widen = jnp.concatenate([upper, lower], 0)
    section_one = jnp.dot(
        spectra.reshape(number * KF, 2 * KF), widen, preferred_element_type=jnp.float32
    )
    section_one = section_one.astype(jnp.bfloat16).reshape(number, KF, 2 * PIX)
    restacked = jnp.concatenate([section_one[:, :, :PIX], section_one[:, :, PIX:]], 1)
    combine = jnp.concatenate([cos_table, -sin_table], 1)
    return jnp.einsum("yk,nkx->nyx", combine, restacked, preferred_element_type=jnp.float32)


def ctf_planes(bin_values):
    freq_index = jnp.arange(KF, dtype=jnp.int32) - KF // 2
    radius = (
        freq_index[:, None] * freq_index[:, None] + freq_index[None, :] * freq_index[None, :]
    ).astype(jnp.float32) / float(KF // 2 * (KF // 2))
    factor = ctf_scale * (1.0 + bin_values / BINS)
    return -jnp.sin(factor[:, None, None] * radius[None, :, :] + amp_phase)


def slot_terms(spectra, chosen, ctf, occupied, cos_table, sin_table):
    image_re = spectra[:, :, :KF].astype(jnp.float32)
    image_im = spectra[:, :, KF:].astype(jnp.float32)
    ref_re = chosen[:, :, :KF].astype(jnp.float32)
    ref_im = chosen[:, :, KF:].astype(jnp.float32)
    cross_re = ctf * (ref_re * image_re + ref_im * image_im)
    cross_im = ctf * (ref_re * image_im - ref_im * image_re)
    cross_term = jnp.concatenate([cross_re, cross_im], 2).astype(jnp.bfloat16)
    ref_power = jnp.sum(ctf * ctf * (ref_re * ref_re + ref_im * ref_im), axis=(1, 2))
    image_power = jnp.sum(image_re * image_re + image_im * image_im, axis=(1, 2))
    scores = (
        inverse(cross_term, cos_table, sin_table)
        * (PIX / jnp.sqrt(ref_power * image_power + 1e-06))[:, None, None]
    )
    weights = jnp.exp(sharpness * (scores - 1.0))
    posterior = (weights / jnp.sum(weights, axis=(1, 2), keepdims=True)).astype(jnp.bfloat16)
    shifts = forward(posterior, cos_table, sin_table)
    shift_re = shifts[:, :, :KF]
    shift_im = shifts[:, :, KF:]
    data_re = PIX * ctf * (shift_re * image_re + shift_im * image_im)
    data_im = PIX * ctf * (shift_re * image_im - shift_im * image_re)
    return jnp.concatenate([data_re, data_im, occupied[:, None, None] * ctf * ctf], 2)


def shell_index(cell_ids):
    coord_x = cell_ids // KF - KF // 2
    coord_y = cell_ids % KF - KF // 2
    depth_pos = jnp.arange(KF, dtype=jnp.int32) - KF // 2
    radius_sq = (coord_x * coord_x + coord_y * coord_y)[:, None] + (depth_pos * depth_pos)[None, :]
    bounds = jnp.arange(1, SHELLS, dtype=jnp.int32)
    return jnp.sum(
        ((bounds * bounds)[None, None, :] <= radius_sq[:, :, None]).astype(jnp.int32), axis=2
    )


def group_count(slot_total):
    wanted = max(1, slot_total // 16)
    for option in range(wanted, 0, -1):
        return option
    return 1


def summed_classes(partial_value):
    return lax.psum(partial_value, "tile").reshape(CLS_DEV * KF, 3 * KF)


def shards(images, references, image_owner, image_class, defocus_bin, slice_cells):
    cos_table, sin_table = dft_tables()
    owners = lax.axis_size("cls")
    tile_count = lax.axis_size("tile")
    my_cls = lax.axis_index("cls")
    my_tile = lax.axis_index("tile")
    local_images = images.shape[0]
    capacity = max(2, 2 * local_images // owners)
    slot_count = owners * capacity
    ref_spectra = forward(references[0], cos_table, sin_table).astype(jnp.bfloat16)
    destination = image_owner[:, 0]
    owner_hits = (destination[:, None] == jnp.arange(owners, dtype=jnp.int32)[None, :]).astype(
        jnp.int32
    )
    before = jnp.cumsum(owner_hits, axis=0) - owner_hits
    position = jnp.sum(before * owner_hits, axis=1)
    slot_of = destination * capacity + position
    chooser = jnp.arange(slot_count, dtype=jnp.int32)[:, None] == slot_of[None, :]
    selector = chooser.astype(jnp.bfloat16)
    class_tag = (
        jnp.sum(jnp.where(chooser, (image_class + 1)[None, :], 0), axis=1)
        .astype(jnp.bfloat16)
        .reshape(owners, capacity)
    )
    bin_tag = (
        jnp.sum(jnp.where(chooser, defocus_bin[None, :], 0), axis=1)
        .astype(jnp.bfloat16)
        .reshape(owners, capacity)
    )
    payload = images.reshape(local_images, PIX * PIX)
    plane_shape = (PIX, PIX)
    packed = jnp.dot(selector, payload, preferred_element_type=jnp.float32).astype(jnp.bfloat16)
    packed = packed.reshape((owners, capacity) + plane_shape)

    def handle(group_data):
        planes, class_part, bin_part = group_data
        spectra = forward(planes, cos_table, sin_table).astype(jnp.bfloat16)
        member = (
            class_part[:, None] == (jnp.arange(CLS_DEV, dtype=jnp.float32) + 1.0)[None, :]
        ).astype(jnp.bfloat16)
        chosen = jnp.einsum(
            "sk,kuv->suv", member, ref_spectra, preferred_element_type=jnp.float32
        ).astype(jnp.bfloat16)
        occupied = (class_part > 0.5).astype(jnp.float32)
        return slot_terms(spectra, chosen, ctf_planes(bin_part), occupied, cos_table, sin_table)

    arrived = lax.all_to_all(packed, "cls", split_axis=0, concat_axis=0, tiled=True)
    class_arrived = lax.all_to_all(class_tag, "cls", split_axis=0, concat_axis=0, tiled=True)
    bin_arrived = lax.all_to_all(bin_tag, "cls", split_axis=0, concat_axis=0, tiled=True)
    sources = arrived.shape[0]
    item_count = arrived.shape[1]
    slot_total = sources * item_count
    groups = group_count(slot_total)
    per_group = slot_total // groups
    grouped = arrived.reshape((groups, per_group) + arrived.shape[2:])
    class_values = class_arrived.reshape(groups, per_group).astype(jnp.float32)
    bin_values = bin_arrived.reshape(groups, per_group).astype(jnp.float32)
    results = lax.map(handle, (grouped, class_values, bin_values))
    contributions = results.reshape(sources, item_count, KF, 3 * KF)
    class_back = class_arrived.astype(jnp.float32)
    member_rows = (
        class_back.reshape(slot_count)[None, :]
        == (jnp.arange(CLS_DEV, dtype=jnp.float32) + 1.0)[:, None]
    ).astype(jnp.float32)
    partial_value = jnp.dot(
        member_rows, contributions.reshape(slot_count, KF * 3 * KF), precision=lax.Precision.HIGHEST
    )
    cells_dev = KF * KF // (owners * tile_count)
    my_block = my_cls * tile_count + my_tile
    flat_cells = slice_cells.reshape(slice_cells.shape[0] * KF)
    owner_rows = CLS_DEV * KF
    my_cells = lax.dynamic_slice_in_dim(flat_cells, my_cls * owner_rows, owner_rows, 0)
    class_sums = summed_classes(partial_value)
    row_ids = jnp.arange(cells_dev * lax.axis_size("cls"), dtype=jnp.int32)
    target = (row_ids // cells_dev * tile_count + my_tile) * cells_dev + row_ids % cells_dev
    onehot = (target[:, None] == my_cells[None, :]).astype(jnp.float32)
    volume = lax.psum_scatter(
        jnp.dot(onehot, class_sums, precision=lax.Precision.HIGHEST),
        "cls",
        scatter_dimension=0,
        tiled=True,
    )
    weight_cols = volume[:, 2 * KF :]
    wiener = volume[:, : 2 * KF] / (jnp.concatenate([weight_cols, weight_cols], 1) + 1.0)
    partner = swapped(wiener.astype(jnp.bfloat16), "half", 0).astype(wiener.dtype)
    shells = shell_index(my_block * cells_dev + jnp.arange(cells_dev, dtype=jnp.int32))
    onehot_shell = (
        shells.reshape(cells_dev * KF)[None, :] == jnp.arange(SHELLS, dtype=jnp.int32)[:, None]
    ).astype(jnp.float32)
    cross_term = (wiener[:, :KF] * partner[:, :KF] + wiener[:, KF:] * partner[:, KF:]).reshape(
        cells_dev * KF
    )
    own_power = (wiener[:, :KF] * wiener[:, :KF] + wiener[:, KF:] * wiener[:, KF:]).reshape(
        cells_dev * KF
    )
    other_power = (partner[:, :KF] * partner[:, :KF] + partner[:, KF:] * partner[:, KF:]).reshape(
        cells_dev * KF
    )
    stacked = jnp.stack([cross_term, own_power, other_power], 0)
    shell_parts = jnp.dot(stacked, onehot_shell.T, precision=lax.Precision.HIGHEST)
    corr_sum, own_sum, other_sum = lax.psum(
        (shell_parts[0], shell_parts[1], shell_parts[2]), ("cls", "tile")
    )
    shell_corr = corr_sum / jnp.maximum(jnp.sqrt(own_sum * other_sum), 1.0)
    positive = jnp.maximum(shell_corr, 0.0)
    shell_weight = jnp.sqrt(2.0 * positive / (1.0 + positive))
    voxel_weight = jnp.dot(
        shell_weight[None, :], onehot_shell, precision=lax.Precision.HIGHEST
    ).reshape(cells_dev, KF)
    return (wiener * jnp.concatenate([voxel_weight, voxel_weight], 1))[None, :, :]


def solution(mesh):
    placed = (
        P(("half", "cls", "tile"), None, None),
        P("half", "cls", None, None),
        P(("half", "cls", "tile"), None),
        P(("half", "cls", "tile")),
        P(("half", "cls", "tile")),
        P(),
    )
    return jax.shard_map(
        shards,
        mesh=mesh,
        in_specs=placed,
        out_specs=P("half", ("cls", "tile"), None),
        check_vma=False,
    )
```

profile of v0, /device:TPU:0, one launch (start us, length us, event | category | flops | bytes accessed | tf_op | source)
XLA Modules:
  0.0 1045.7 jit_solution(14953446340479506018)
XLA Ops:
  6.5 0.8 fusion.88
  7.4 0.8 select_reduce_fusion.2
  8.9 0.7 select_reduce_fusion.1
  9.6 0.7 convert_element_type.238
  10.4 9.8 all-to-all-start
  20.1 0.7 convert_element_type.239
  20.9 6.6 copy.55
  27.4 2.5 all-to-all-done
  29.9 7.3 all-to-all-start.1
  37.2 7.9 convolution_convert_fusion.4
  45.1 8.9 copy.56
  54.0 9.9 all-to-all-start.2
  68.6 179.2 %all-to-all-done.2 = bf16[32,2,256,256]{3,2,1,0:T(8,128)(2,1)} async-done(((bf16[32,2,256,256]{3,2,1,0:T(8,128)(2,1)}), bf16[32,2,256,256]{3,2,1,0:T(8,128)(2,1)}, u32[]{:S(2)}, u32[]{:S(2)}) %all-to-all-start.2) | async-done | bytes 8388640 | tf_op jit(solution)/shard_map/all_to_all | solution.py:175
  247.8 129.8 %while.12 = (s32[]{:T(128)}, f32[4,16,128,384]{3,2,1,0:T(8,128)}, f32[4,16]{1,0:T(4,128)S(1)}, f32[4,16]{1,0:T(4,128)S(1)}, bf16[2,128,256]{2,0,1:T(2,128)(2,1)S...) while((s32[]{:T(128)}, f32[4,16,128,384]{3,2,1,0:T(8,128)}, ...), condition=%wide.region_8.9_spmd, body=%wide.region_4.8_spmd.sunk | while | flops 3258237184 | bytes 95619848 | solution.py:186
  248.0 1.7 constant_dynamic-slice_fusion.4
  250.4 0.7 fusion.157
  251.1 2.4 copy.71
  254.7 4.5 fusion.159
  260.6 1.4 fusion.161
  262.0 1.0 divide_convert_fusion.2
  263.6 2.7 fusion.162
  266.4 5.4 copy.74
  271.8 5.6 fusion.163
  277.7 2.6 copy_dynamic-update-slice_fusion.2
  280.3 1.7 constant_dynamic-slice_fusion.4
  283.5 2.4 copy.71
  287.1 4.5 fusion.159
  292.9 1.4 fusion.161
  294.3 1.0 divide_convert_fusion.2
  296.0 2.7 fusion.162
  298.7 5.4 copy.74
  304.2 5.6 fusion.163
  310.0 2.7 copy_dynamic-update-slice_fusion.2
  312.7 1.7 constant_dynamic-slice_fusion.4
  315.9 2.4 copy.71
  319.5 4.5 fusion.159
  325.3 1.4 fusion.161
  326.7 1.0 divide_convert_fusion.2
  328.4 2.7 fusion.162
  331.1 5.4 copy.74
  336.6 5.6 fusion.163
  342.4 2.7 copy_dynamic-update-slice_fusion.2
  345.1 1.7 constant_dynamic-slice_fusion.4
  348.3 2.4 copy.71
  351.9 4.5 fusion.159
  357.7 1.4 fusion.161
  359.1 1.0 divide_convert_fusion.2
  360.8 2.7 fusion.162
  363.5 5.4 copy.74
  369.0 5.6 fusion.163
  374.8 2.6 copy_dynamic-update-slice_fusion.2
  377.6 16.1 %copy.57 = f32[8,8,128,384]{3,1,2,0:T(8,128)} copy(f32[8,8,128,384]{3,2,1,0:T(8,128)} %bitcast.146) | data formatting | bytes 25165824
  393.8 7.1 fusion.90
  400.9 1.1 reshape.322
  402.0 0.8 dynamic_slice.23
  402.8 49.7 %all-reduce.3.cloned.1.call-done = f32[256,384]{1,0:T(8,128)} async-done(((f32[256,384]{1,0:T(8,128)}), f32[256,384]{1,0:T(8,128)}) %all-reduce.3.cloned.1.call-update) | async-done | bytes 393232 | tf_op jit(solution)/shard_map/psum | solution.py:126
  452.5 7.0 fusion.43
  459.6 224.4 %reduce-scatter.2.cloned.1.call-done = f32[128,384]{1,0:T(8,128)} async-done(((f32[4096,384]{1,0:T(8,128)}), f32[128,384]{1,0:T(8,128)}) %reduce-scatter.2.cloned.1.call-update) | async-done | bytes 196624 | tf_op jit(solution)/shard_map/reduce_scatter | solution.py:205
  684.0 0.8 slice.161
  684.9 0.9 fusion.112
  686.6 0.8 collective-permute-done
  687.4 2.1 fusion.45
  689.6 346.8 %all-reduce = (f32[64]{0:T(128)S(1)}, f32[64]{0:T(128)S(1)}, f32[64]{0:T(128)S(1)}) all-reduce(f32[64]{0:T(128)S(1)} %get-tuple-element.227, f32[64]{0:T(128)S(1)} %get-tuple-element.226, f32[64]{0:T(128)S(1)} %get-tuple-element.225), channel_id=1, replica_groups=mesh['half'=2,'cls'=32,'tile'=4] {'cls','tile'}, use_global_device_ids=true, to_apply=%region_12.13 | all-reduce | flops 192 | bytes 1536 | tf_op jit(solution)/shard_map/psum | solution.py:229
  1036.4 1.4 fusion.46
  (111 shorter events, 25.1 us)
Async XLA Ops:
  6.5 58.6 %copy-start = (bf16[1,2,256,256]{3,2,1,0:T(8,128)(2,1)S(1)}, bf16[1,2,256,256]{3,2,1,0:T(8,128)(2,1)}, u32[]{:S(2)}) copy-start(bf16[1,2,256,256]{3,2,1,0:T(8,128)(2,1)} %param.9) | copy-start | bytes 786436
  10.4 19.5 %all-to-all-start = ((bf16[32,1,2]{2,1,0:T(2,128)(2,1)}), bf16[32,1,2]{2,1,0:T(2,128)(2,1)S(1)}, u32[]{:S(2)}, u32[]{:S(2)}) async-start(bf16[32,1,2]{2,1,0:T(2,128)(2,1)} %convert_element_type.238), calls=%async_computation | async-start | bytes 32768 | tf_op jit(solution)/shard_map/all_to_all | solution.py:176
  29.9 24.1 %all-to-all-start.1 = ((bf16[32,1,2]{2,1,0:T(2,128)(2,1)}), bf16[32,1,2]{2,1,0:T(2,128)(2,1)S(1)}, u32[]{:S(2)}, u32[]{:S(2)}) async-start(bf16[32,1,2]{2,1,0:T(2,128)(2,1)} %convert_element_type.239), calls=%async_computation.1 | async-start | bytes 32768 | tf_op jit(solution)/shard_map/all_to_all | solution.py:177
  54.0 193.8 %all-to-all-start.2 = ((bf16[32,2,256,256]{3,2,1,0:T(8,128)(2,1)}), bf16[32,2,256,256]{3,2,1,0:T(8,128)(2,1)}, u32[]{:S(2)}, u32[]{:S(2)}) async-start(bf16[32,2,256,256]{3,2,1,0:T(8,128)(2,1)} %bitcast.143), calls=%async_computation.2 | async-start | bytes 16777216 | tf_op jit(solution)/shard_map/all_to_all | solution.py:175
  63.9 388.6 %all-reduce.3.cloned.1.call-start = ((), (), s32[]{:S(2)}) async-start(), calls=%async_computation.4 | async-start | bytes 786432 | tf_op jit(solution)/shard_map/psum | solution.py:126
  377.6 16.2 %copy-start.2 = (f32[64]{0:T(128)S(1)}, f32[64]{0:T(128)}, u32[]{:S(2)}) copy-start(f32[64]{0:T(128)} %reshape.323) | copy-start | bytes 772
  377.6 16.2 %copy-start.3 = (f32[2]{0:T(128)S(1)}, f32[2]{0:T(128)}, u32[]{:S(2)}) copy-start(f32[2]{0:T(128)} %iota_add_fusion.2) | copy-start | bytes 28
  402.0 282.1 %reduce-scatter.2.cloned.1.call-start = ((), (), s32[]{:S(2)}) async-start(), calls=%async_computation.5 | async-start | bytes 6488064 | tf_op jit(solution)/shard_map/reduce_scatter | solution.py:205
  459.5 578.9 %copy-start.1 = (bf16[1,2,256,256]{3,2,1,0:T(8,128)(2,1)S(1)}, bf16[1,2,256,256]{3,2,1,0:T(8,128)(2,1)}, u32[]{:S(2)}) copy-start(bf16[1,2,256,256]{3,2,1,0:T(8,128)(2,1)} %param.9) | copy-start | bytes 786436
  685.8 1.6 collective-permute-start
Sparse Core Ops, SparseCore 0:
  402.1 50.3 all-reduce.2
  459.6 224.3 reduce-scatter.1
where the time goes:
time: 1050 us
  waiting for transfers between devices  457 us (44%)
  blocking collectives  347 us (33%)
  local copies, waits for them, and re-layouts  87.8 us (8%)
  matrix products  56.2 us (5%)
  other arithmetic  55.9 us (5%)
  starting transfers between devices  27.4 us (3%)
  between operations  14.1 us (1%)
    psum x1, blocking collectives, shards(): lax.psum((shell_parts[0], shell_parts[1], shell_parts[2]), ('cls', 'tile'))  347 us
    reduce_scatter x1, waiting for transfers between devices, shards(): lax.psum_scatter(jnp.dot(onehot, class_sums, precision=lax.Precision.HIGH...  224 us
    all_to_all x1, waiting for transfers between devices, shards(): lax.all_to_all(packed, 'cls', split_axis=0, concat_axis=0, tiled=True)  179 us
    psum x1, waiting for transfers between devices, summed_classes(): return lax.psum(partial_value, 'tile').reshape(CLS_DEV * KF, 3 * KF)  49.7 us
    unnamed x11, local copies, waits for them, and re-layouts  31.6 us
    dot_general x8, local copies, waits for them, and re-layouts, forward(): jnp.einsum('kp,npq->nkq', stacked, section_one, preferred_element_type=jn...  31.5 us
    mul x4, other arithmetic, slot_terms(): data_re = PIX * ctf * (shift_re * image_re + shift_im * image_im)  22.5 us
  transfers between devices with their start and end apart: 6, of which 5 were waited for; matrix products, arithmetic and copies ran while one was open for 3% of the time, Pallas kernels for 0%

commit v1 on v0

v1 whole, which is shorter than its diff:
```python
import functools
import math

import jax
import jax.numpy as jnp
import numpy as np
from jax import lax
from jax.experimental import pallas as pl
from jax.experimental.pallas import tpu as pltpu
from jax.sharding import PartitionSpec as P

PIX = 256
KF = 128
HK = 64
CLS_DEV = 2
BINS = 16
SHELLS = 64
NY, NZ, NX = 4, 8, 4
OWNERS = NY * NZ
ROWS = 144
PR = 80
PA = 48
GROUP = 4

sharpness = 40.0
ctf_scale = 6.0
amp_phase = 0.1

MESH = pl.DeviceIdType.MESH
BF = jnp.bfloat16
F32 = jnp.float32


def dft_tables():
    sample_pos = np.arange(PIX, dtype=np.int32)[:, None]
    freq_pos = np.arange(KF, dtype=np.int32)[None, :] - KF // 2
    angles = (sample_pos * freq_pos % PIX).astype(np.float32) * np.float32(2.0 * math.pi / PIX)
    scaling = np.float32(1.0 / math.sqrt(PIX))
    bf = jnp.bfloat16
    return (np.cos(angles) * scaling).astype(bf), (np.sin(angles) * scaling).astype(bf)


def ctf_table():
    freq = np.arange(KF, dtype=np.int32) - KF // 2
    radius = (freq[:, None] * freq[:, None] + freq[None, :] * freq[None, :]).astype(
        np.float32
    ) / np.float32(HK * HK)
    factor = (ctf_scale * (1.0 + np.arange(BINS) / BINS)).astype(np.float32)
    return -np.sin(factor[:, None, None] * radius[None] + np.float32(amp_phase)).astype(np.float32)


def expand_tables():
    turn = np.zeros((256, 256), np.float32)
    column = np.zeros((256, 256), np.float32)
    middle = np.zeros((256, 256), np.float32)
    for c in range(1, KF):
        turn[c, KF - c] = 1.0
        turn[KF + c, 2 * KF - c] = -1.0
    column[:KF, 0] = 1.0
    column[KF:, KF] = 1.0
    for c in range(HK + 1):
        middle[c, c] = 1.0
        middle[KF + c, KF + c] = 1.0
    for c in range(1, HK):
        middle[c, KF - c] = 1.0
        middle[KF + c, 2 * KF - c] = -1.0
    return np.concatenate([turn, column, middle], 0)


def row_turn():
    turn = np.zeros((HK, HK), np.float32)
    for r in range(1, HK):
        turn[r, HK - r] = 1.0
    return turn


def dot(a, b):
    return jnp.dot(a, b, preferred_element_type=F32)


def pick(chooser, rows):
    high = rows.astype(BF)
    return dot(chooser, high) + dot(chooser, (rows - high.astype(F32)).astype(BF))


def transform(plane, cs, cst):
    section = dot(plane, cs).astype(BF)
    both = dot(cst, section)
    real = both[:KF, :KF] - both[KF:, KF:]
    imag = -(both[KF:, :KF] + both[:KF, KF:])
    return real, imag


def left_over(part):
    low = part[HK:, :]
    row = lax.broadcasted_iota(jnp.int32, (HK, KF), 0)
    col = lax.broadcasted_iota(jnp.int32, (HK, KF), 1)
    line = jnp.sum(jnp.where((col == row + HK) & (row > 0), low[:, 0:1], 0.0), axis=0, keepdims=True)
    first = lax.broadcasted_iota(jnp.int32, (1, KF), 1) <= HK
    return jnp.where(first, low[0:1, :], line)


def lower_masks(rows):
    row = lax.broadcasted_iota(jnp.int32, (rows, 2 * KF), 0) % KF
    col = lax.broadcasted_iota(jnp.int32, (rows, 2 * KF), 1) % KF
    return (row > HK) & (col == row), (row == HK) & (col <= HK)


def here():
    half, cls, tile = lax.axis_index("half"), lax.axis_index("cls"), lax.axis_index("tile")
    y, z = cls // NZ, cls % NZ

    def at(dy=0, dz=0, dx=0):
        return (half, (y + dy) % NY * NZ + (z + dz) % NZ, (tile + dx) % NX)

    return half, y, z, tile, at


def remote(src, dst, send, recv, device):
    return pltpu.make_async_remote_copy(
        src_ref=src, dst_ref=dst, send_sem=send, recv_sem=recv, device_id=device, device_id_type=MESH
    )


def greet(devices):
    barrier = pltpu.get_barrier_semaphore()
    for device in devices:
        pl.semaphore_signal(barrier, inc=1, device_id=device, device_id_type=MESH)
    pl.semaphore_wait(barrier, len(devices))


GATHER_SEMS = 72


def gather_kernel(plane_ref, cs_ref, cst_ref, g_ref, own_ref, send_sem, recv_sem):
    _, y, z, tile, at = here()
    greet([at(dz=1), at(dz=-1), at(dy=1), at(dy=-1), at(dx=1), at(dx=-1)])
    line = lax.broadcasted_iota(jnp.int32, (16, KF), 0)
    tail_re = jnp.zeros((16, KF), F32)
    tail_im = jnp.zeros((16, KF), F32)
    for k in range(CLS_DEV):
        real, imag = transform(plane_ref[k], cs_ref[...], cst_ref[...])
        own_ref[k * HK : (k + 1) * HK, 0:KF] = real[:HK].astype(BF)
        own_ref[k * HK : (k + 1) * HK, KF : 2 * KF] = imag[:HK].astype(BF)
        tail_re = jnp.where(line == k, left_over(real), tail_re)
        tail_im = jnp.where(line == k, left_over(imag), tail_im)
    own_ref[128:144, 0:KF] = tail_re.astype(BF)
    own_ref[128:144, KF : 2 * KF] = tail_im.astype(BF)

    sent = []

    def copy(i, view, device):
        ref = g_ref.at[view]
        return remote(ref, ref, send_sem.at[i], recv_sem.at[i], device)

    def push(view, device):
        i = len(sent)
        out = copy(i, view, device)
        out.start()
        sent.append(out)
        return i

    def take(i, view):
        copy(i, view, at(dz=1)).wait_recv()

    def along(dx):
        return pl.ds(pl.multiple_of(PR + 16 * ((tile + dx) % NX), 16), 16)

    whole, front, back = pl.ds(0, PR), pl.ds(0, PA), pl.ds(PA, PR - PA)
    every, low, high = pl.ds(0, NZ), pl.ds(0, NZ // 2), pl.ds(NZ // 2, NZ // 2)
    mine = along(0)
    g_ref[y, z, whole, :] = own_ref[whole, :]
    g_ref[y, z, mine, :] = own_ref[mine, :]
    up, down = at(dz=1), at(dz=-1)
    north, south = at(dy=1), at(dy=-1)
    east, west = at(dx=1), at(dx=-1)
    yw, ye, yo = (y - 1) % NY, (y + 1) % NY, (y + 2) % NY

    r_up, r_down = push((y, z, mine), up), push((y, z, mine), down)
    p_up, p_down = push((y, z, whole), up), push((y, z, whole), down)
    waiting, last = [], []

    def cross(zz):
        waiting.append((zz, push((y, zz, whole), north), push((y, zz, whole), south)))

    def settle():
        zz, a, b = waiting.pop(0)
        take(a, (yw, zz, whole))
        fa = push((yw, zz, front), north)
        take(b, (ye, zz, whole))
        fb = push((ye, zz, back), south)
        last.append((zz, fa, fb))

    cross(z)
    for d in range(1, 5):
        zm, zp = (z - d) % NZ, (z + d) % NZ
        take(r_up, (y, zm, mine))
        if d < 4:
            r_up = push((y, zm, mine), up)
            take(r_down, (y, zp, mine))
        if d < 3:
            r_down = push((y, zp, mine), down)
        if d == 4:
            a, b = push((y, every, mine), north), push((y, every, mine), south)
        take(p_up, (y, zm, whole if d < 4 else front))
        if d < 4:
            p_up = push((y, zm, whole if d < 3 else front), up)
        take(p_down, (y, zp, whole if d < 4 else back))
        if d < 4:
            p_down = push((y, zp, whole if d < 3 else back), down)
            cross(zm)
        cross(zp)
        settle()

    def spread(yy):
        return yy, push((yy, every, mine), east), push((yy, every, mine), west)

    x_wait, x_last = [spread(y)], []

    def x_settle():
        yy, p, q = x_wait.pop(0)
        take(p, (yy, every, along(-1)))
        fp = push((yy, low, along(-1)), east)
        take(q, (yy, every, along(1)))
        fq = push((yy, high, along(1)), west)
        x_last.append((yy, fp, fq))

    take(a, (yw, every, mine))
    fa = push((yw, low, mine), north)
    x_wait.append(spread(yw))
    take(b, (ye, every, mine))
    fb = push((ye, high, mine), south)
    x_wait.append(spread(ye))
    settle()
    take(fa, (yo, low, mine))
    take(fb, (yo, high, mine))
    x_wait.append(spread(yo))
    while waiting or x_wait:
        if x_wait:
            x_settle()
        if waiting:
            settle()
    for zz, fa, fb in last:
        take(fa, (yo, zz, front))
        take(fb, (yo, zz, back))
    for yy, fp, fq in x_last:
        take(fp, (yy, low, along(2)))
        take(fq, (yy, high, along(2)))
    for out in sent:
        out.wait_send()


def image_kernel(
    owner_ref, class_ref, bin_ref, img_ref, refs_ref, ctf_ref, cs_ref, cst_ref, widen_ref,
    combine_ref, expand_ref, turn_ref, out_ref, acc_ref,
):
    step = pl.program_id(0)

    @pl.when(step == 0)
    def _():
        acc_ref[...] = jnp.zeros_like(acc_ref)

    cs, cst = cs_ref[...], cst_ref[...]
    diag, mid = lower_masks(KF)
    diag, mid = diag[HK:], mid[HK:]
    row8 = lax.broadcasted_iota(jnp.int32, (8, 2 * KF), 0)
    col8 = lax.broadcasted_iota(jnp.int32, (8, 2 * KF), 1)

    loaded = []
    for g in range(GROUP):
        n = step * GROUP + g
        o, k, b = owner_ref[n], class_ref[n], bin_ref[n]
        im_re, im_im = transform(img_ref[g], cs, cst)
        im_re, im_im = im_re.astype(BF).astype(F32), im_im.astype(BF).astype(F32)
        top = refs_ref[o, pl.ds(pl.multiple_of(k * HK, HK), HK), :]
        tail = refs_ref[o, 128:144, :].astype(F32)
        extra = jnp.where(k > 0, tail[1:2, :], tail[0:1, :])
        back = dot(top, expand_ref[0:256, :]).astype(BF)
        fill = jnp.concatenate(
            [jnp.where(diag, extra, 0.0).astype(BF), jnp.where(mid, extra, 0.0).astype(BF)], 1
        )
        low = dot(turn_ref[...], back) + dot(fill, expand_ref[256:768, :])
        full = jnp.concatenate([top.astype(F32), low], 0)
        ref_re, ref_im = full[:, :KF], full[:, KF:]
        ctf = ctf_ref[b]
        cross_re = ctf * (ref_re * im_re + ref_im * im_im)
        cross_im = ctf * (ref_re * im_im - ref_im * im_re)
        crossed = jnp.concatenate([cross_re, cross_im], 1).astype(BF)
        ref_power = jnp.sum(ctf * ctf * (ref_re * ref_re + ref_im * ref_im), keepdims=True)
        image_power = jnp.sum(im_re * im_re + im_im * im_im, keepdims=True)
        scale = (PIX * sharpness) / jnp.sqrt(ref_power * image_power + 1e-06)
        loaded.append((o, k, b, im_re, im_im, ctf, crossed, scale))
    ends = []
    for g in range(GROUP):
        o, k, b, im_re, im_im, ctf, crossed, scale = loaded[g]
        inner = dot(crossed, widen_ref[...]).astype(BF)
        stacked = jnp.concatenate([inner[:, :PIX], inner[:, PIX:]], 0)
        scores = dot(combine_ref[...], stacked)
        weights = jnp.exp(scores * scale - sharpness)
        total = jnp.sum(weights, keepdims=True)
        posterior = (weights * (1.0 / total)).astype(BF)
        sh_re, sh_im = transform(posterior, cs, cst)
        ctf = PIX * ctf
        data_re = ctf * (sh_re * im_re + sh_im * im_im)
        data_im = ctf * (sh_re * im_im - sh_im * im_re)
        ends.append((o, k, b, data_re, data_im))
    for g in range(GROUP):
        o, k, b, data_re, data_im = ends[g]
        rows = pl.ds(pl.multiple_of(k * HK, HK), HK)
        acc_ref[o, rows, 0:KF] += data_re[:HK]
        acc_ref[o, rows, KF : 2 * KF] += data_im[:HK]
        extra = jnp.concatenate([left_over(data_re), left_over(data_im)], 1)
        count = jnp.where((row8 == 2) & (col8 == k * BINS + b), 1.0, 0.0)
        acc_ref[o, 128:136, :] += jnp.where(row8 == k, extra, count)

    @pl.when(step == pl.num_programs(0) - 1)
    def _():
        out_ref[...] = acc_ref[...].astype(BF)


REDUCE_SEMS = 160
Z_ORDER = (4, 3, 5, 2, 6, 1, 7, 0)


def reduce_kernel(
    d_ref, ctf_ref, slot_ref, cell_ref, expand_ref, left_ref, o_ref,
    pin_p, pin_m, ps_p, ps_m, pr_p, pr_m, pz_s, pz_r, px_s, px_r,
    rin_p, rin_m, rs_p, rs_m, rr_p, rr_m, ry_s, ry_r, rz_s, rz_r, rx_s, rx_r,
    held, sb, rb, wz_s, wz_r, sz_s, sz_r, sy_s, sy_r, sx_s, sx_r, bins,
    send_sem, recv_sem,
):
    half, y, z, tile, at = here()
    cls = y * NZ + z
    north, south = at(dy=1), at(dy=-1)
    east, west = at(dx=1), at(dx=-1)
    twin = (1 - half, cls, tile)

    def owner_at(k):
        return (half, (cls + k) % OWNERS, tile)

    greet([owner_at(k) for k in range(1, OWNERS)] + [at(dx=k) for k in (1, 2, 3)] + [twin])
    sent = []

    def push(src, dst, device):
        i = len(sent)
        out = remote(src, dst, send_sem.at[i], recv_sem.at[i], device)
        out.start()
        sent.append(out)
        return i

    def take(i, dst):
        remote(dst, dst, send_sem.at[i], recv_sem.at[i], east).wait_recv()

    def along(dx):
        return pl.ds(pl.multiple_of(PR + 16 * ((tile + dx) % NX), 16), 16)

    def f(v):
        return v.astype(F32)

    yn, ys, yo = (y + 1) % NY, (y - 1) % NY, (y + 2) % NY
    front, back, whole = pl.ds(0, PA), pl.ds(PA, PR - PA), pl.ds(0, PR)
    every = pl.ds(0, NZ)
    first_p, first_r = {}, {}
    for n, j in enumerate(Z_ORDER):
        zz = (z + j) % NZ
        first_p[j] = (
            push(d_ref.at[yo, zz, front], pin_p.at[j], north),
            push(d_ref.at[yo, zz, back], pin_m.at[j], south),
        )
        if n % 2 == 0:
            yy = n // 2
            if yy < 2:
                first_r[yy] = push(d_ref.at[yy, every, along(2)], rin_p.at[yy], east)
            else:
                first_r[yy] = push(d_ref.at[yy, every, along(2)], rin_m.at[yy - 2], west)
    second_p, second_r = {}, {}
    for n, j in enumerate(Z_ORDER):
        zz = (z + j) % NZ
        a, b = first_p[j]
        take(a, pin_p.at[j])
        ps_p[j, 0:PA] = (f(d_ref[yn, zz, 0:PA]) + f(pin_p[j])).astype(BF)
        ps_p[j, PA:PR] = d_ref[yn, zz, PA:PR]
        a = push(ps_p.at[j], pr_p.at[j], north)
        take(b, pin_m.at[j])
        ps_m[j, 0:PA] = d_ref[ys, zz, 0:PA]
        ps_m[j, PA:PR] = (f(d_ref[ys, zz, PA:PR]) + f(pin_m[j])).astype(BF)
        b = push(ps_m.at[j], pr_m.at[j], south)
        second_p[j] = a, b
        if n % 2 == 0:
            yy = n // 2
            if yy < 2:
                take(first_r[yy], rin_p.at[yy])
                rs_p[yy] = (f(d_ref[yy, every, along(1)]) + f(rin_p[yy])).astype(BF)
                rs_m[yy] = d_ref[yy, every, along(-1)]
            else:
                take(first_r[yy], rin_m.at[yy - 2])
                rs_p[yy] = d_ref[yy, every, along(1)]
                rs_m[yy] = (f(d_ref[yy, every, along(-1)]) + f(rin_m[yy - 2])).astype(BF)
            second_r[yy] = (
                push(rs_p.at[yy], rr_p.at[yy], east),
                push(rs_m.at[yy], rr_m.at[yy], west),
            )
    third_p = {}
    for n, j in enumerate(Z_ORDER):
        zz = (z + j) % NZ
        a, b = second_p[j]
        take(a, pr_p.at[j])
        take(b, pr_m.at[j])
        pz_s[j] = (f(d_ref[y, zz, 0:PR]) + f(pr_p[j]) + f(pr_m[j])).astype(BF)
        if j:
            third_p[j] = push(pz_s.at[j], pz_r.at[j], at(dz=j))
        if n % 2 == 0:
            yy = n // 2
            a, b = second_r[yy]
            take(a, rr_p.at[yy])
            take(b, rr_m.at[yy])
            ry_s[yy] = (f(d_ref[yy, every, along(0)]) + f(rr_p[yy]) + f(rr_m[yy])).astype(BF)
    third_r = {k: push(ry_s.at[(y + k) % NY], ry_r.at[k], at(dy=k)) for k in (2, 1, 3)}
    total = f(ry_s[y])
    for k in (1, 2, 3):
        take(third_r[k], ry_r.at[k])
        total = total + f(ry_r[k])
    rz_s[...] = total.astype(BF)
    fourth_r = {j: push(rz_s.at[(z + j) % NZ], rz_r.at[j], at(dz=j)) for j in Z_ORDER[:-1]}
    total = f(pz_s[0])
    for j in range(1, NZ):
        take(third_p[j], pz_r.at[j])
        total = total + f(pz_r[j])
    px_s[...] = total
    fourth_p = {k: push(px_s, px_r.at[k], at(dx=k)) for k in (1, 2, 3)}
    total = f(rz_s[z])
    for j in range(1, NZ):
        take(fourth_r[j], rz_r.at[j])
        total = total + f(rz_r[j])
    rx_s[...] = total
    fifth_r = {k: push(rx_s, rx_r.at[k], at(dx=k)) for k in (1, 2, 3)}
    total = px_s[...]
    for k in (1, 2, 3):
        take(fourth_p[k], px_r.at[k])
        total = total + px_r[k]
    held[0:PR] = total
    held[along(0), :] = rx_s[...]
    for k in (1, 2, 3):
        take(fifth_r[k], rx_r.at[k])
        held[along(-k), :] = rx_r[k]

    sums = held[...]
    spread = pick(left_ref[...], sums)
    diag, mid = lower_masks(2 * KF)
    extra = spread[512:768]
    parts = jnp.concatenate(
        [spread[256:512], jnp.where(diag, extra, 0.0), jnp.where(mid, extra, 0.0)], 1
    )
    high = parts.astype(BF)
    rest = (parts - f(high)).astype(BF)
    data = spread[0:256] + dot(high, expand_ref[...]) + dot(rest, expand_ref[...])
    counts = sums[128:144]
    weights = []
    for k in range(CLS_DEV):
        weight = jnp.zeros((KF, KF), F32)
        for b in range(BINS):
            ctf = ctf_ref[b]
            weight = weight + counts[2:3, k * BINS + b : k * BINS + b + 1] * (ctf * ctf)
        weights.append(weight)
    weight = jnp.concatenate(weights, 0)
    place = lax.broadcasted_iota(jnp.int32, (OWNERS * 16, 2 * KF), 0)
    slot = slot_ref[...]
    packed = jnp.zeros((OWNERS * 16, KF), F32)
    for c, piece in enumerate((data[:, :KF], data[:, KF:], weight)):
        chooser = jnp.where(place == slot + 4 * c, 1.0, 0.0).astype(BF)
        packed = packed + pick(chooser, piece)
    sb[...] = packed.reshape(OWNERS, 16, KF)
    rb[cls] = sb[cls]
    used = pl.ds(0, 12)
    went = {
        k: push(sb.at[(cls + k) % OWNERS, used], rb.at[cls, used], owner_at(k)) for k in range(1, OWNERS)
    }
    for k in range(1, OWNERS):
        rb[(cls - k) % OWNERS, 12:16] = jnp.zeros((4, KF), F32)
        take(went[k], rb.at[(cls - k) % OWNERS, used])

    arrived = rb[...].reshape(OWNERS * 16, KF)
    cell = lax.broadcasted_iota(jnp.int32, (KF, OWNERS * 16), 0)
    kind = lax.broadcasted_iota(jnp.int32, (KF, OWNERS * 16), 1) % 16 // 4
    hit = cell == cell_ref[...]
    volume = [pick(jnp.where(hit & (kind == c), 1.0, 0.0).astype(BF), arrived) for c in range(3)]
    scale = 1.0 / (volume[2] + 1.0)
    w_re, w_im = volume[0] * scale, volume[1] * scale
    wz_s[:, 0:KF] = w_re.astype(BF)
    wz_s[:, KF : 2 * KF] = w_im.astype(BF)
    i = push(wz_s, wz_r, twin)
    d0 = lax.broadcasted_iota(jnp.int32, (KF, KF), 0) - HK
    d1 = lax.broadcasted_iota(jnp.int32, (KF, KF), 1) - HK
    plane = cls * NX + tile - HK
    radius = plane * plane + d0 * d0 + d1 * d1
    own = w_re * w_re + w_im * w_im
    take(i, wz_r)
    o_re, o_im = f(wz_r[:, 0:KF]), f(wz_r[:, KF : 2 * KF])
    both = w_re * o_re + w_im * o_im
    other = o_re * o_re + o_im * o_im

    for s in range(SHELLS):
        inside = radius >= s * s
        if s < SHELLS - 1:
            inside = inside & (radius < (s + 1) * (s + 1))
        for q, v in enumerate((both, own, other)):
            part = jnp.where(inside, v, 0.0).reshape(KF // 8, 8, KF)
            bins[q, s * 8 : s * 8 + 8, :] = jnp.sum(part, axis=0)
    line = lax.broadcasted_iota(jnp.int32, (8, KF), 0)
    ones = jnp.ones((8, KF), F32)
    group = lax.broadcasted_iota(jnp.int32, (SHELLS * 8, KF), 0) // 8
    group = jnp.where(group == lax.broadcasted_iota(jnp.int32, (SHELLS * 8, KF), 1), 1.0, 0.0)
    sums = jnp.zeros((8, KF), F32)
    for q in range(3):
        part = lax.dot_general(
            ones, bins[q], (((1,), (1,)), ((), ())), precision=lax.Precision.HIGHEST,
            preferred_element_type=F32,
        )
        part = jnp.dot(part, group, precision=lax.Precision.HIGHEST, preferred_element_type=F32)
        sums = jnp.where(line == q, part, sums)
    for s_ref, r_ref, devices in (
        (sz_s, sz_r, {j: at(dz=j) for j in Z_ORDER[:-1]}),
        (sy_s, sy_r, {k: at(dy=k) for k in (2, 1, 3)}),
        (sx_s, sx_r, {k: at(dx=k) for k in (2, 1, 3)}),
    ):
        s_ref[...] = sums
        tags = {k: push(s_ref, r_ref.at[k], device) for k, device in devices.items()}
        for k, tag in tags.items():
            take(tag, r_ref.at[k])
            sums = sums + r_ref[k]
    fsc = sums[0:1] / jnp.maximum(jnp.sqrt(sums[1:2] * sums[2:3]), 1.0)
    fsc = jnp.maximum(fsc, 0.0)
    gain = jnp.sqrt(2.0 * fsc / (1.0 + fsc))
    voxel = jnp.zeros((KF, KF), F32)
    for s in range(SHELLS):
        voxel = jnp.where(radius >= s * s, gain[:, s : s + 1], voxel)
    o_ref[0, :, 0:KF] = w_re * voxel
    o_ref[0, :, KF : 2 * KF] = w_im * voxel
    for out in sent:
        out.wait_send()


def left_table():
    table = np.zeros((768, ROWS), np.float32)
    for k in range(CLS_DEV):
        for r in range(KF):
            if r < HK:
                table[k * KF + r, k * HK + r] = 1.0
            elif r > HK:
                table[256 + k * KF + r, k * HK + KF - r] = 1.0
            table[512 + k * KF + r, 2 * HK + k] = 1.0
    return table


def routes(slice_cells):
    cls, tile = lax.axis_index("cls"), lax.axis_index("tile")
    cells = slice_cells.reshape(OWNERS, CLS_DEV * KF)
    block = cells // KF
    own = lax.dynamic_index_in_dim(block, cls, 0, keepdims=False)
    entry = jnp.arange(CLS_DEV * KF, dtype=jnp.int32)
    same = (own[:, None] == own[None, :]) & (entry[:, None] < entry[None, :])
    rank = jnp.sum(same.astype(jnp.int32), axis=0)
    slot = jnp.where(own % NX == tile, own // NX * 16 + rank, -4096)[None, :]
    mine = block == cls * NX + tile
    strict = jnp.asarray(np.triu(np.ones((256, 256), np.float32), 1), BF)
    before = dot(mine.astype(BF), strict).astype(jnp.int32)
    want = mine[:, None, :] & (before[:, None, :] == jnp.arange(4, dtype=jnp.int32)[None, :, None])
    cell = jnp.sum(jnp.where(want, cells[:, None, :] % KF + 1, 0), axis=2) - 1
    empty = jnp.full((OWNERS, 4), -1, jnp.int32)
    return slot, jnp.concatenate([cell, cell, cell, empty], 1).reshape(1, OWNERS * 16)


def shards(images, references, image_owner, image_class, defocus_bin, slice_cells):
    cos_table, sin_table = dft_tables()
    cs = jnp.asarray(np.concatenate([cos_table, sin_table], 1))
    cst = jnp.asarray(np.concatenate([cos_table.T, sin_table.T], 0))
    widen = jnp.asarray(
        np.concatenate(
            [
                np.concatenate([cos_table.T, sin_table.T], 1),
                np.concatenate([-sin_table.T, cos_table.T], 1),
            ],
            0,
        )
    )
    combine = jnp.asarray(np.concatenate([cos_table, -sin_table], 1))
    ctf = jnp.asarray(ctf_table())
    expand = jnp.asarray(expand_tables(), BF)
    turn = jnp.asarray(row_turn(), BF)
    left = jnp.asarray(left_table(), BF)
    local = images.shape[0]
    vmem = pl.BlockSpec(memory_space=pltpu.VMEM)
    dma = pltpu.SemaphoreType.DMA

    spectra = pl.pallas_call(
        gather_kernel,
        name="gather_references",
        out_shape=jax.ShapeDtypeStruct((NY, NZ, ROWS, 2 * KF), BF),
        in_specs=[vmem] * 3,
        out_specs=vmem,
        scratch_shapes=[
            pltpu.VMEM((ROWS, 2 * KF), BF), dma((GATHER_SEMS,)), dma((GATHER_SEMS,)),
        ],
        compiler_params=pltpu.CompilerParams(
            collective_id=0, has_side_effects=True, vmem_limit_bytes=32 << 20
        ),
    )(references[0], cs, cst)

    def fixed(shape):
        return pl.BlockSpec(shape, lambda i, *_: (0,) * len(shape))

    partial = pl.pallas_call(
        image_kernel,
        name="image_terms",
        out_shape=jax.ShapeDtypeStruct((OWNERS, ROWS, 2 * KF), BF),
        grid_spec=pltpu.PrefetchScalarGridSpec(
            num_scalar_prefetch=3,
            grid=(local // GROUP,),
            in_specs=[
                pl.BlockSpec((GROUP, PIX, PIX), lambda i, *_: (i, 0, 0)),
                fixed((OWNERS, ROWS, 2 * KF)),
                fixed((BINS, KF, KF)),
                fixed((PIX, 2 * KF)),
                fixed((2 * KF, PIX)),
                fixed((2 * KF, 2 * PIX)),
                fixed((PIX, 2 * KF)),
                fixed((768, 256)),
                fixed((HK, HK)),
            ],
            out_specs=fixed((OWNERS, ROWS, 2 * KF)),
            scratch_shapes=[pltpu.VMEM((OWNERS, ROWS, 2 * KF), F32)],
        ),
        compiler_params=pltpu.CompilerParams(
            dimension_semantics=("arbitrary",), vmem_limit_bytes=48 << 20
        ),
    )(
        image_owner[:, 0], image_class, defocus_bin, images,
        spectra.reshape(OWNERS, ROWS, 2 * KF), ctf, cs, cst, widen, combine, expand, turn,
    )

    slot, cell = routes(slice_cells)

    def buf(*shape):
        return pltpu.VMEM(shape, BF)

    wide = 2 * KF
    return pl.pallas_call(
        reduce_kernel,
        name="reduce_maps",
        out_shape=jax.ShapeDtypeStruct((1, KF, 2 * KF), F32),
        in_specs=[vmem] * 6,
        out_specs=vmem,
        scratch_shapes=[
            buf(NZ, PA, wide), buf(NZ, PR - PA, wide),
            buf(NZ, PR, wide), buf(NZ, PR, wide), buf(NZ, PR, wide), buf(NZ, PR, wide),
            buf(NZ, PR, wide), buf(NZ, PR, wide), pltpu.VMEM((PR, wide), F32), pltpu.VMEM((NX, PR, wide), F32),
            buf(2, NZ, 16, wide), buf(2, NZ, 16, wide),
            buf(NY, NZ, 16, wide), buf(NY, NZ, 16, wide), buf(NY, NZ, 16, wide), buf(NY, NZ, 16, wide),
            buf(NY, NZ, 16, wide), buf(NY, NZ, 16, wide), buf(NZ, 16, wide), buf(NZ, 16, wide),
            pltpu.VMEM((16, wide), F32), pltpu.VMEM((NX, 16, wide), F32),
            pltpu.VMEM((ROWS, wide), F32), pltpu.VMEM((OWNERS, 16, KF), F32), pltpu.VMEM((OWNERS, 16, KF), F32),
            buf(KF, wide), buf(KF, wide),
            pltpu.VMEM((8, KF), F32), pltpu.VMEM((NZ, 8, KF), F32),
            pltpu.VMEM((8, KF), F32), pltpu.VMEM((NY, 8, KF), F32),
            pltpu.VMEM((8, KF), F32), pltpu.VMEM((NX, 8, KF), F32), pltpu.VMEM((3, SHELLS * 8, KF), F32),
            dma((REDUCE_SEMS,)), dma((REDUCE_SEMS,)),
        ],
        compiler_params=pltpu.CompilerParams(
            collective_id=1, has_side_effects=True, vmem_limit_bytes=40 << 20
        ),
    )(partial.reshape(NY, NZ, ROWS, 2 * KF), ctf, slot, cell, expand, left)


def solution(mesh):
    placed = (
        P(("half", "cls", "tile"), None, None),
        P("half", "cls", None, None),
        P(("half", "cls", "tile"), None),
        P(("half", "cls", "tile")),
        P(("half", "cls", "tile")),
        P(),
    )
    return jax.shard_map(
        shards,
        mesh=mesh,
        in_specs=placed,
        out_specs=P("half", ("cls", "tile"), None),
        check_vma=False,
    )
```

time: 1050 us -> 135 us (0.13)
  the two profiles are of different devices: /device:TPU:0 before, /device:TPU:1 now
where the time goes in v1:
time: 135 us; the launch traced here: 134 us
  Pallas kernels  125 us (93%)
  local copies, waits for them, and re-layouts  7.18 us (5%)
    pallas_call x1, Pallas kernels, shards(): pl.pallas_call(reduce_kernel, name='reduce_maps', out_shape=jax.ShapeDtyp...  60.4 us
    pallas_call x1, Pallas kernels, shards(): pl.pallas_call(gather_kernel, name='gather_references', out_shape=jax.Sha...  32.7 us
    pallas_call x1, Pallas kernels, shards(): pl.pallas_call(image_kernel, name='image_terms', out_shape=jax.ShapeDtype...  32.4 us
    unnamed x36, local copies, waits for them, and re-layouts  7 us

profile of v1, /device:TPU:1, one launch (start us, length us, event | category | flops | bytes accessed | tf_op | source)
XLA Modules:
  0.0 134.3 jit_solution(18195994641377989854)
XLA Ops:
  0.0 0.0 copy-start.1
  0.0 0.0 copy-start.2
  0.0 0.0 copy-start.4
  0.0 1.0 copy-done.4
  1.0 0.0 copy-start.6
  1.0 0.9 copy-done.6
  1.9 0.0 copy-start.10
  1.9 0.9 copy-done.10
  2.9 0.0 copy-start.5
  2.9 0.0 copy-start.7
  2.9 0.0 copy-start.9
  2.9 0.0 copy-start.11
  2.9 0.0 copy-start.12
  2.9 0.0 copy-start.13
  2.9 0.0 copy-start.14
  2.9 0.0 copy-start.15
  2.9 32.7 %gather_references.1 = bf16[4,8,144,256]{3,2,1,0:T(8,128)(2,1)S(1)} custom-call(bf16[2,256,256]{2,1,0:T(8,128)(2,1)S(1)} %bitcast.10, bf16[256,256]{1,0:T(8,128)(2,1)S(1)} %copy-done.4, bf16[256,256]{1,0:T(8,128)(2,1)S(1)} %copy-done.6), custom_call_target="tpu_custom_call" | custom-call | tf_op jit(solution)/shard_map/gather_references/pallas_call | solution.py:595
  35.6 0.0 copy-start
  35.6 1.4 %copy-done = bf16[4,8,144,256]{3,2,1,0:T(8,128)(2,1)} copy-done((bf16[4,8,144,256]{3,2,1,0:T(8,128)(2,1)}, bf16[4,8,144,256]{3,2,1,0:T(8,128)(2,1)S(1)}, u32[]{:S(2)}) %copy-start) | copy-done | bytes 2359320
  37.1 0.0 copy-done.1
  37.1 0.0 copy-done.2
  37.1 0.0 copy-done.5
  37.1 0.0 copy-done.7
  37.1 0.0 copy-done.9
  37.1 0.0 copy-done.11
  37.1 0.0 copy-done.12
  37.1 0.0 copy-done.13
  37.1 0.0 copy-done.14
  37.1 0.0 copy-done.15
  37.1 0.0 copy-start.16
  37.1 32.4 %image_terms.1 = bf16[32,144,256]{2,1,0:T(8,128)(2,1)S(1)} custom-call(s32[32]{0:T(128)S(1)} %bitcast.11, s32[32]{0:T(128)S(1)} %copy-done.14, s32[32]{0:T(128)S(1)} %copy-done.15, bf16[32,256,256]{2,1,0:T(8,128)(2,1)} %img_ref.1, bf16[32,144,256]{2,1,0:T(8,128)(2,1)} %bitcast.9, f32[16,128,128]{2,1,0:T(8,128)S(1)} %copy-done.1, ...), custom_call_target="tpu_custom_call" | custom-call | tf_op jit(solution)/shard_map/image_terms/pallas_call | solution.py:612
  69.5 0.0 copy-done.16
  69.6 0.1 convert_reduce_fusion
  69.8 1.0 convolution_convert_fusion
  70.9 0.2 select_reduce_fusion
  71.1 0.1 copy.16
  71.1 0.1 reshape.78.cell_ref
  71.2 0.0 copy-start.3
  71.2 1.0 copy-done.3
  72.2 0.0 copy-start.8
  72.2 1.0 copy-done.8
  73.2 60.4 %reduce_maps.1 = f32[1,128,256]{2,1,0:T(8,128)S(1)} custom-call(bf16[4,8,144,256]{3,2,1,0:T(8,128)(2,1)S(1)} %bitcast.8, f32[16,128,128]{2,1,0:T(8,128)S(1)} %copy-done.1, s32[1,256]{1,0:T(1,128)S(1)} %compare_select_fusion.slot_ref, s32[1,512]{1,0:T(1,128)S(1)} %reshape.78.cell_ref, bf16[768,256]{1,0:T(8,128)(2,1)S(1)} %copy-done.3, ...), custom_call_target="tpu_custom_call" | custom-call | tf_op jit(solution)/shard_map/reduce_maps/pallas_call | solution.py:647
  133.6 0.7 copy.21
  (9 shorter events, 0.1 us)
Async XLA Ops:
  0.0 37.1 %copy-start.1 = (f32[16,128,128]{2,1,0:T(8,128)S(1)}, f32[16,128,128]{2,1,0:T(8,128)}, u32[]{:S(2)}) copy-start(f32[16,128,128]{2,1,0:T(8,128)} %constant.98.clone.ctf_ref) | copy-start | bytes 3145732
  0.0 37.1 %copy-start.2 = (bf16[768,256]{1,0:T(8,128)(2,1)S(1)}, bf16[768,256]{1,0:T(8,128)(2,1)}, u32[]{:S(2)}) copy-start(bf16[768,256]{1,0:T(8,128)(2,1)} %constant.99.clone.expand_ref) | copy-start | bytes 1179652
  0.0 1.0 copy-start.4
  1.0 0.9 copy-start.6
  1.9 0.9 copy-start.10
  2.9 34.2 %copy-start.5 = (bf16[256,256]{1,0:T(8,128)(2,1)S(1)}, bf16[256,256]{1,0:T(8,128)(2,1)}, u32[]{:S(2)}) copy-start(bf16[256,256]{1,0:T(8,128)(2,1)} %constant.94.clone.cs_ref) | copy-start | bytes 393220
  2.9 34.2 %copy-start.7 = (bf16[256,256]{1,0:T(8,128)(2,1)S(1)}, bf16[256,256]{1,0:T(8,128)(2,1)}, u32[]{:S(2)}) copy-start(bf16[256,256]{1,0:T(8,128)(2,1)} %constant.95.clone.cst_ref) | copy-start | bytes 393220
  2.9 34.2 %copy-start.9 = (bf16[256,512]{1,0:T(8,128)(2,1)S(1)}, bf16[256,512]{1,0:T(8,128)(2,1)}, u32[]{:S(2)}) copy-start(bf16[256,512]{1,0:T(8,128)(2,1)} %constant.96.clone.widen_ref) | copy-start | bytes 786436
  2.9 34.2 %copy-start.11 = (bf16[256,256]{1,0:T(8,128)(2,1)S(1)}, bf16[256,256]{1,0:T(8,128)(2,1)}, u32[]{:S(2)}) copy-start(bf16[256,256]{1,0:T(8,128)(2,1)} %constant.97.clone.combine_ref) | copy-start | bytes 393220
  2.9 34.2 %copy-start.12 = (bf16[64,64]{1,0:T(8,128)(2,1)S(1)}, bf16[64,64]{1,0:T(8,128)(2,1)}, u32[]{:S(2)}) copy-start(bf16[64,64]{1,0:T(8,128)(2,1)} %constant.100.clone.turn_ref) | copy-start | bytes 24580
  2.9 34.2 %copy-start.13 = (s32[32,1]{0,1:T(1,128)S(1)}, s32[32,1]{0,1:T(1,128)}, u32[]{:S(2)}) copy-start(s32[32,1]{0,1:T(1,128)} %param.17) | copy-start | bytes 388
  2.9 34.2 %copy-start.14 = (s32[32]{0:T(128)S(1)}, s32[32]{0:T(128)}, u32[]{:S(2)}) copy-start(s32[32]{0:T(128)} %class_ref.1) | copy-start | bytes 388
  2.9 34.2 %copy-start.15 = (s32[32]{0:T(128)S(1)}, s32[32]{0:T(128)}, u32[]{:S(2)}) copy-start(s32[32]{0:T(128)} %bin_ref.1) | copy-start | bytes 388
  35.6 1.4 %copy-start = (bf16[4,8,144,256]{3,2,1,0:T(8,128)(2,1)}, bf16[4,8,144,256]{3,2,1,0:T(8,128)(2,1)S(1)}, u32[]{:S(2)}) copy-start(bf16[4,8,144,256]{3,2,1,0:T(8,128)(2,1)S(1)} %gather_references.1) | copy-start | bytes 7077892
  37.1 32.4 %copy-start.16 = (s32[64,128]{1,0:T(8,128)S(1)}, s32[64,128]{1,0:T(8,128)}, u32[]{:S(2)}) copy-start(s32[64,128]{1,0:T(8,128)} %param.20) | copy-start | bytes 98308
  71.2 1.0 copy-start.3
  72.2 1.0 copy-start.8

commit v2 on v1

v2 whole, which is shorter than its diff:
```python
import functools
import math

import jax
import jax.numpy as jnp
import numpy as np
from jax import lax
from jax.experimental import pallas as pl
from jax.experimental.pallas import tpu as pltpu
from jax.sharding import PartitionSpec as P

PIX = 256
KF = 128
HK = 64
CLS_DEV = 2
BINS = 16
SHELLS = 64
NY, NZ, NX = 4, 8, 4
OWNERS = NY * NZ
ROWS = 144
PR = 80
PA = 48
GROUP = 8

sharpness = 40.0
ctf_scale = 6.0
amp_phase = 0.1

MESH = pl.DeviceIdType.MESH
BF = jnp.bfloat16
F32 = jnp.float32


def dft_tables():
    sample_pos = np.arange(PIX, dtype=np.int32)[:, None]
    freq_pos = np.arange(KF, dtype=np.int32)[None, :] - KF // 2
    angles = (sample_pos * freq_pos % PIX).astype(np.float32) * np.float32(2.0 * math.pi / PIX)
    scaling = np.float32(1.0 / math.sqrt(PIX))
    bf = jnp.bfloat16
    return (np.cos(angles) * scaling).astype(bf), (np.sin(angles) * scaling).astype(bf)


def ctf_table():
    freq = np.arange(KF, dtype=np.int32) - KF // 2
    radius = (freq[:, None] * freq[:, None] + freq[None, :] * freq[None, :]).astype(
        np.float32
    ) / np.float32(HK * HK)
    factor = (ctf_scale * (1.0 + np.arange(BINS) / BINS)).astype(np.float32)
    return -np.sin(factor[:, None, None] * radius[None] + np.float32(amp_phase)).astype(np.float32)


def expand_tables():
    turn = np.zeros((256, 256), np.float32)
    column = np.zeros((256, 256), np.float32)
    middle = np.zeros((256, 256), np.float32)
    for c in range(1, KF):
        turn[c, KF - c] = 1.0
        turn[KF + c, 2 * KF - c] = -1.0
    column[:KF, 0] = 1.0
    column[KF:, KF] = 1.0
    for c in range(HK + 1):
        middle[c, c] = 1.0
        middle[KF + c, KF + c] = 1.0
    for c in range(1, HK):
        middle[c, KF - c] = 1.0
        middle[KF + c, 2 * KF - c] = -1.0
    return np.concatenate([turn, column, middle], 0)


def row_turn():
    turn = np.zeros((HK, HK), np.float32)
    for r in range(1, HK):
        turn[r, HK - r] = 1.0
    return turn


def dot(a, b):
    return jnp.dot(a, b, preferred_element_type=F32)


def pick(chooser, rows):
    high = rows.astype(BF)
    return dot(chooser, high) + dot(chooser, (rows - high.astype(F32)).astype(BF))


def transform(plane, cs, cst):
    section = dot(plane, cs).astype(BF)
    both = dot(cst, section)
    real = both[:KF, :KF] - both[KF:, KF:]
    imag = -(both[KF:, :KF] + both[:KF, KF:])
    return real, imag


def left_over(part):
    low = part[HK:, :]
    row = lax.broadcasted_iota(jnp.int32, (HK, KF), 0)
    col = lax.broadcasted_iota(jnp.int32, (HK, KF), 1)
    line = jnp.sum(jnp.where((col == row + HK) & (row > 0), low[:, 0:1], 0.0), axis=0, keepdims=True)
    first = lax.broadcasted_iota(jnp.int32, (1, KF), 1) <= HK
    return jnp.where(first, low[0:1, :], line)


def lower_masks(rows):
    row = lax.broadcasted_iota(jnp.int32, (rows, 2 * KF), 0) % KF
    col = lax.broadcasted_iota(jnp.int32, (rows, 2 * KF), 1) % KF
    return (row > HK) & (col == row), (row == HK) & (col <= HK)


def here():
    half, cls, tile = lax.axis_index("half"), lax.axis_index("cls"), lax.axis_index("tile")
    y, z = cls // NZ, cls % NZ

    def at(dy=0, dz=0, dx=0):
        return (half, (y + dy) % NY * NZ + (z + dz) % NZ, (tile + dx) % NX)

    return half, y, z, tile, at


def remote(src, dst, send, recv, device):
    return pltpu.make_async_remote_copy(
        src_ref=src, dst_ref=dst, send_sem=send, recv_sem=recv, device_id=device, device_id_type=MESH
    )


def greet(devices):
    barrier = pltpu.get_barrier_semaphore()
    for device in devices:
        pl.semaphore_signal(barrier, inc=1, device_id=device, device_id_type=MESH)
    pl.semaphore_wait(barrier, len(devices))


GATHER_SEMS = 80


def gather_kernel(
    plane_any, table_any, g_ref, plane_ref, table_ref, own_ref, copy_sem, send_sem, recv_sem
):
    loads = [
        pltpu.make_async_copy(plane_any, plane_ref, copy_sem.at[0]),
        pltpu.make_async_copy(table_any, table_ref, copy_sem.at[1]),
    ]
    for load in loads:
        load.start()
    _, y, z, tile, at = here()
    greet([at(dz=k) for k in range(1, NZ)] + [at(dy=1), at(dy=-1), at(dx=1), at(dx=-1)])
    for load in loads:
        load.wait()
    line = lax.broadcasted_iota(jnp.int32, (16, KF), 0)
    tail_re = jnp.zeros((16, KF), F32)
    tail_im = jnp.zeros((16, KF), F32)
    for k in range(CLS_DEV):
        real, imag = transform(plane_ref[k], table_ref[0:PIX, :], table_ref[PIX : 2 * PIX, :])
        own_ref[k * HK : (k + 1) * HK, 0:KF] = real[:HK].astype(BF)
        own_ref[k * HK : (k + 1) * HK, KF : 2 * KF] = imag[:HK].astype(BF)
        tail_re = jnp.where(line == k, left_over(real), tail_re)
        tail_im = jnp.where(line == k, left_over(imag), tail_im)
    own_ref[128:144, 0:KF] = tail_re.astype(BF)
    own_ref[128:144, KF : 2 * KF] = tail_im.astype(BF)

    sent = []

    def copy(i, view, device):
        ref = g_ref.at[view]
        return remote(ref, ref, send_sem.at[i], recv_sem.at[i], device)

    def push(view, device):
        i = len(sent)
        out = copy(i, view, device)
        out.start()
        sent.append(out)
        return i

    def take(i, view):
        copy(i, view, at(dz=1)).wait_recv()

    def along(dx):
        return pl.ds(pl.multiple_of(PR + 16 * ((tile + dx) % NX), 16), 16)

    whole, front, back = pl.ds(0, PR), pl.ds(0, PA), pl.ds(PA, PR - PA)
    every, low, high = pl.ds(0, NZ), pl.ds(0, NZ // 2), pl.ds(NZ // 2, NZ // 2)
    mine = along(0)
    g_ref[y, z, whole, :] = own_ref[whole, :]
    g_ref[y, z, mine, :] = own_ref[mine, :]
    up, down = at(dz=1), at(dz=-1)
    north, south = at(dy=1), at(dy=-1)
    east, west = at(dx=1), at(dx=-1)
    yw, ye, yo = (y - 1) % NY, (y + 1) % NY, (y + 2) % NY

    r_tags = {j: push((y, z, mine), at(dz=j)) for j in (4, 3, 5, 2, 6, 1, 7)}
    p_up, p_down = push((y, z, whole), up), push((y, z, whole), down)
    waiting, last = [], []

    def cross(zz):
        waiting.append((zz, push((y, zz, whole), north), push((y, zz, whole), south)))

    def settle():
        zz, a, b = waiting.pop(0)
        take(a, (yw, zz, whole))
        fa = push((yw, zz, front), north)
        take(b, (ye, zz, whole))
        fb = push((ye, zz, back), south)
        last.append((zz, fa, fb))

    def spread(yy):
        return yy, push((yy, every, mine), east), push((yy, every, mine), west)

    x_wait, x_last = [], []

    def x_settle():
        yy, p, q = x_wait.pop(0)
        take(p, (yy, every, along(-1)))
        fp = push((yy, low, along(-1)), east)
        take(q, (yy, every, along(1)))
        fq = push((yy, high, along(1)), west)
        x_last.append((yy, fp, fq))

    cross(z)
    for j, tag in r_tags.items():
        take(tag, (y, (z - j) % NZ, mine))
    ra, rb = push((y, every, mine), north), push((y, every, mine), south)
    x_wait.append(spread(y))
    for d in range(1, 5):
        zm, zp = (z - d) % NZ, (z + d) % NZ
        take(p_up, (y, zm, whole if d < 4 else front))
        if d < 4:
            p_up = push((y, zm, whole if d < 3 else front), up)
        take(p_down, (y, zp, whole if d < 4 else back))
        if d < 4:
            p_down = push((y, zp, whole if d < 3 else back), down)
            cross(zm)
        cross(zp)
        if d == 1:
            take(ra, (yw, every, mine))
            fa = push((yw, low, mine), north)
            x_wait.append(spread(yw))
            take(rb, (ye, every, mine))
            fb = push((ye, high, mine), south)
            x_wait.append(spread(ye))
        elif d == 2:
            take(fa, (yo, low, mine))
            take(fb, (yo, high, mine))
            x_wait.append(spread(yo))
        else:
            x_settle()
        settle()
    while waiting or x_wait:
        if waiting:
            settle()
        if x_wait:
            x_settle()
    for zz, fa, fb in last:
        take(fa, (yo, zz, front))
        take(fb, (yo, zz, back))
    for yy, fp, fq in x_last:
        take(fp, (yy, low, along(2)))
        take(fq, (yy, high, along(2)))
    for out in sent:
        out.wait_send()


def image_kernel(
    owner_ref, class_ref, bin_ref, img_ref, refs_ref, ctf_ref, cs_ref, cst_ref, widen_ref,
    combine_ref, expand_ref, turn_ref, out_ref, acc_ref,
):
    step = pl.program_id(0)

    @pl.when(step == 0)
    def _():
        acc_ref[...] = jnp.zeros_like(acc_ref)

    cs, cst = cs_ref[...], cst_ref[...]
    diag, mid = lower_masks(KF)
    diag, mid = diag[HK:], mid[HK:]
    row8 = lax.broadcasted_iota(jnp.int32, (8, 2 * KF), 0)
    col8 = lax.broadcasted_iota(jnp.int32, (8, 2 * KF), 1)

    def halves(section):
        both = dot(cst, section)
        return both[:KF, :KF] - both[KF:, KF:], -(both[KF:, :KF] + both[:KF, KF:])

    section = dot(img_ref[...].reshape(GROUP * PIX, PIX), cs).astype(BF)
    which = [(owner_ref[step * GROUP + g], class_ref[step * GROUP + g], bin_ref[step * GROUP + g]) for g in range(GROUP)]
    tops = [refs_ref[o, pl.ds(pl.multiple_of(k * HK, HK), HK), :] for o, k, _ in which]
    backs = dot(jnp.concatenate(tops, 0), expand_ref[0:256, :]).astype(BF)
    fills = []
    for o, k, _ in which:
        tail = refs_ref[o, 128:144, :].astype(F32)
        extra = jnp.where(k > 0, tail[1:2, :], tail[0:1, :])
        fills.append(jnp.concatenate(
            [jnp.where(diag, extra, 0.0).astype(BF), jnp.where(mid, extra, 0.0).astype(BF)], 1
        ))
    filled = dot(jnp.concatenate(fills, 0), expand_ref[256:768, :])
    loaded, crosses = [], []
    for g in range(GROUP):
        o, k, b = which[g]
        im_re, im_im = halves(section[g * PIX : (g + 1) * PIX])
        im_re, im_im = im_re.astype(BF).astype(F32), im_im.astype(BF).astype(F32)
        low = dot(turn_ref[...], backs[g * HK : (g + 1) * HK]) + filled[g * HK : (g + 1) * HK]
        full = jnp.concatenate([tops[g].astype(F32), low], 0)
        ref_re, ref_im = full[:, :KF], full[:, KF:]
        ctf = ctf_ref[b]
        cross_re = ctf * (ref_re * im_re + ref_im * im_im)
        cross_im = ctf * (ref_re * im_im - ref_im * im_re)
        crosses.append(jnp.concatenate([cross_re, cross_im], 1).astype(BF))
        ref_power = jnp.sum(ctf * ctf * (ref_re * ref_re + ref_im * ref_im), keepdims=True)
        image_power = jnp.sum(im_re * im_re + im_im * im_im, keepdims=True)
        scale = (PIX * sharpness) / jnp.sqrt(ref_power * image_power + 1e-06)
        loaded.append((im_re, im_im, scale))
    inner = dot(jnp.concatenate(crosses, 0), widen_ref[...]).astype(BF)
    posteriors = []
    for g in range(GROUP):
        part = inner[g * KF : (g + 1) * KF]
        stacked = jnp.concatenate([part[:, :PIX], part[:, PIX:]], 0)
        scores = dot(combine_ref[...], stacked)
        weights = jnp.exp(scores * loaded[g][2] - sharpness)
        total = jnp.sum(weights, keepdims=True)
        posteriors.append((weights * (1.0 / total)).astype(BF))
    section = dot(jnp.concatenate(posteriors, 0), cs).astype(BF)
    for g in range(GROUP):
        o, k, b = which[g]
        im_re, im_im, _ = loaded[g]
        sh_re, sh_im = halves(section[g * PIX : (g + 1) * PIX])
        ctf = PIX * ctf_ref[b]
        data_re = ctf * (sh_re * im_re + sh_im * im_im)
        data_im = ctf * (sh_re * im_im - sh_im * im_re)
        rows = pl.ds(pl.multiple_of(k * HK, HK), HK)
        acc_ref[o, rows, 0:KF] += data_re[:HK]
        acc_ref[o, rows, KF : 2 * KF] += data_im[:HK]
        extra = jnp.concatenate([left_over(data_re), left_over(data_im)], 1)
        count = jnp.where((row8 == 2) & (col8 == k * BINS + b), 1.0, 0.0)
        acc_ref[o, 128:136, :] += jnp.where(row8 == k, extra, count)

    @pl.when(step == pl.num_programs(0) - 1)
    def _():
        out_ref[...] = acc_ref[...].astype(BF)


REDUCE_SEMS = 160
Z_ORDER = (4, 3, 5, 2, 6, 1, 7, 0)


def routes(cells, cls, tile):
    cells = cells.astype(F32)
    row = lax.broadcasted_iota(jnp.int32, (OWNERS, 2 * OWNERS), 0)
    col = lax.broadcasted_iota(jnp.int32, (OWNERS, 2 * OWNERS), 1)
    pair = [
        pick(jnp.where(col == 2 * row + k, 1.0, 0.0).astype(BF), cells) for k in range(CLS_DEV)
    ]
    cells = jnp.concatenate(pair, 1).astype(jnp.int32)
    block = lax.shift_right_arithmetic(cells, 7)
    inner = (cells - block * KF + 1).astype(F32)
    first = lax.broadcasted_iota(jnp.int32, (256, 256), 0)
    second = lax.broadcasted_iota(jnp.int32, (256, 256), 1)
    mine = block == cls * NX + tile
    strict = jnp.where(first < second, 1.0, 0.0).astype(BF)
    before = dot(jnp.where(mine, 1.0, 0.0).astype(BF), strict)
    owner = lax.broadcasted_iota(jnp.int32, (OWNERS, OWNERS * 16), 0)
    lane = lax.broadcasted_iota(jnp.int32, (OWNERS, OWNERS * 16), 1)
    here_ = (lax.shift_right_arithmetic(lane, 4) == owner) & ((lane & 15) < 12)
    table = jnp.zeros((OWNERS, OWNERS * 16), F32)
    for r in range(4):
        cell = jnp.sum(jnp.where(mine & (before == r), inner, 0.0), axis=1, keepdims=True)
        table = jnp.where(here_ & ((lane & 3) == r), cell, table)
    cell = (jnp.sum(table, axis=0, keepdims=True) - 1.0).astype(jnp.int32)
    owner = lax.broadcasted_iota(jnp.int32, (OWNERS, 256), 0)
    own = jnp.sum(jnp.where(owner == cls, block.astype(F32), 0.0), axis=0, keepdims=True)
    turned = jnp.sum(jnp.where(first == second, own, 0.0), axis=1, keepdims=True)
    same = jnp.where((turned == own) & (first < second), 1.0, 0.0)
    rank = jnp.sum(same, axis=0, keepdims=True).astype(jnp.int32)
    own = own.astype(jnp.int32)
    slot = lax.shift_right_arithmetic(own, 2) * 16 + rank
    return jnp.where((own & 3) == tile, slot, -4096), cell


def reduce_kernel(
    d_ref, ctf_ref, cells_ref, expand_any, left_any, o_ref,
    expand_ref, left_ref, pin_p, pin_m, ps_p, ps_m, pr_p, pr_m, pz_s, pz_r, px_s, px_r,
    rin_p, rin_m, rs_p, rs_m, rr_p, rr_m, ry_s, ry_r, rz_s, rz_r, rx_s, rx_r,
    held, sb, rb, wz_s, wz_r, sz_s, sz_r, sx_s, sx_r, bins,
    copy_sem, send_sem, recv_sem,
):
    half, y, z, tile, at = here()
    cls = y * NZ + z
    north, south = at(dy=1), at(dy=-1)
    east, west = at(dx=1), at(dx=-1)
    twin = (1 - half, cls, tile)

    def owner_at(k):
        return (half, (cls + k) % OWNERS, tile)

    tables = [
        pltpu.make_async_copy(expand_any, expand_ref, copy_sem.at[0]),
        pltpu.make_async_copy(left_any, left_ref, copy_sem.at[1]),
    ]
    for table in tables:
        table.start()
    plane_peers = {
        (dy, dx): at(dy=dy, dx=dx) for dy in (2, 1, 3, 0) for dx in (2, 1, 3, 0) if dy or dx
    }
    greet(
        [owner_at(k) for k in range(1, OWNERS)]
        + [device for (dy, dx), device in plane_peers.items() if dx]
        + [twin]
    )
    sent = []

    def push(src, dst, device):
        i = len(sent)
        out = remote(src, dst, send_sem.at[i], recv_sem.at[i], device)
        out.start()
        sent.append(out)
        return i

    def take(i, dst):
        remote(dst, dst, send_sem.at[i], recv_sem.at[i], east).wait_recv()

    def along(dx):
        return pl.ds(pl.multiple_of(PR + 16 * ((tile + dx) % NX), 16), 16)

    def f(v):
        return v.astype(F32)

    yn, ys, yo = (y + 1) % NY, (y - 1) % NY, (y + 2) % NY
    front, back = pl.ds(0, PA), pl.ds(PA, PR - PA)
    every = pl.ds(0, NZ)
    first_p, first_r = {}, {}
    for n, j in enumerate(Z_ORDER):
        zz = (z + j) % NZ
        if n < NY:
            if n < 2:
                first_r[n] = push(d_ref.at[n, every, along(2)], rin_p.at[n], east)
            else:
                first_r[n] = push(d_ref.at[n, every, along(2)], rin_m.at[n - 2], west)
        first_p[j] = (
            push(d_ref.at[yo, zz, front], pin_p.at[j], north),
            push(d_ref.at[yo, zz, back], pin_m.at[j], south),
        )
    plain_p, plain_r = {}, {}
    for n, j in enumerate(Z_ORDER):
        zz = (z + j) % NZ
        if n < NY:
            if n < 2:
                plain_r[n] = push(d_ref.at[n, every, along(-1)], rr_m.at[n], west)
            else:
                plain_r[n] = push(d_ref.at[n, every, along(1)], rr_p.at[n], east)
        plain_p[j] = (
            push(d_ref.at[yn, zz, back], pr_p.at[j, back], north),
            push(d_ref.at[ys, zz, front], pr_m.at[j, front], south),
        )

    slot, cell = routes(cells_ref[...], cls, tile)
    place = lax.broadcasted_iota(jnp.int32, (OWNERS * 16, 2 * KF), 0)
    chooser = jnp.concatenate(
        [jnp.where(place == slot + 4 * c, 1.0, 0.0).astype(BF) for c in range(3)], 1
    )

    second_p, second_r = {}, {}
    for n, j in enumerate(Z_ORDER):
        zz = (z + j) % NZ
        if n < NY:
            if n < 2:
                take(first_r[n], rin_p.at[n])
                rs_p[n] = (f(d_ref[n, every, along(1)]) + f(rin_p[n])).astype(BF)
                second_r[n] = push(rs_p.at[n], rr_p.at[n], east)
            else:
                take(first_r[n], rin_m.at[n - 2])
                rs_m[n - 2] = (f(d_ref[n, every, along(-1)]) + f(rin_m[n - 2])).astype(BF)
                second_r[n] = push(rs_m.at[n - 2], rr_m.at[n], west)
        a, b = first_p[j]
        take(a, pin_p.at[j])
        ps_p[j] = (f(d_ref[yn, zz, front]) + f(pin_p[j])).astype(BF)
        a = push(ps_p.at[j], pr_p.at[j, front], north)
        take(b, pin_m.at[j])
        ps_m[j] = (f(d_ref[ys, zz, back]) + f(pin_m[j])).astype(BF)
        b = push(ps_m.at[j], pr_m.at[j, back], south)
        second_p[j] = a, b

    third_p = {}

    def settle(j):
        zz = (z + j) % NZ
        a, b = plain_p[j]
        take(a, pr_p.at[j, back])
        take(b, pr_m.at[j, front])
        a, b = second_p[j]
        take(a, pr_p.at[j, front])
        take(b, pr_m.at[j, back])
        pz_s[j] = (f(d_ref[y, zz, pl.ds(0, PR)]) + f(pr_p[j]) + f(pr_m[j])).astype(BF)
        if j:
            third_p[j] = push(pz_s.at[j], pz_r.at[j], at(dz=j))

    for n, j in enumerate(Z_ORDER[:4]):
        settle(j)
        take(second_r[n], (rr_p if n < 2 else rr_m).at[n])
        take(plain_r[n], (rr_m if n < 2 else rr_p).at[n])
        ry_s[n] = (f(d_ref[n, every, along(0)]) + f(rr_p[n]) + f(rr_m[n])).astype(BF)
    third_r = {k: push(ry_s.at[(y + k) % NY], ry_r.at[k], at(dy=k)) for k in (2, 1, 3)}
    for j in Z_ORDER[4:6]:
        settle(j)
    total = f(ry_s[y])
    for k in (1, 2, 3):
        take(third_r[k], ry_r.at[k])
        total = total + f(ry_r[k])
    rz_s[...] = total.astype(BF)
    fourth_r = {j: push(rz_s.at[(z + j) % NZ], rz_r.at[j], at(dz=j)) for j in Z_ORDER[:-1]}
    for j in Z_ORDER[6:]:
        settle(j)

    d0 = lax.broadcasted_iota(jnp.int32, (KF, KF), 0) - HK
    d1 = lax.broadcasted_iota(jnp.int32, (KF, KF), 1) - HK
    plane = cls * NX + tile - HK
    radius = plane * plane + d0 * d0 + d1 * d1
    shell = jnp.zeros((KF, KF), jnp.int32)
    for s in range(1, SHELLS):
        shell = jnp.where(radius >= s * s, s, shell)

    total = f(rz_s[z])
    for j in range(1, NZ):
        take(fourth_r[j], rz_r.at[j])
        total = total + f(rz_r[j])
    rx_s[...] = total
    fifth_r = {k: push(rx_s, rx_r.at[k], at(dx=k)) for k in (2, 1, 3)}
    total = f(pz_s[0])
    for j in range(1, NZ):
        take(third_p[j], pz_r.at[j])
        total = total + f(pz_r[j])
    px_s[...] = total
    fourth_p = {k: push(px_s, px_r.at[k], at(dx=k)) for k in (2, 1, 3)}
    held[along(0), :] = rx_s[...]
    for k in (1, 2, 3):
        take(fifth_r[k], rx_r.at[k])
        held[along(-k), :] = rx_r[k]
    counts = held[128:144]
    weights = []
    for k in range(CLS_DEV):
        weight = jnp.zeros((KF, KF), F32)
        for b in range(BINS):
            ctf = ctf_ref[b]
            weight = weight + counts[2:3, k * BINS + b : k * BINS + b + 1] * (ctf * ctf)
        weights.append(weight)
    for table in tables:
        table.wait()
    total = px_s[...]
    for k in (1, 2, 3):
        take(fourth_p[k], px_r.at[k])
        total = total + px_r[k]
    held[0:PR] = total

    sums = held[...]
    spread = pick(left_ref[...], sums)
    diag, mid = lower_masks(2 * KF)
    extra = spread[512:768]
    parts = jnp.concatenate(
        [spread[256:512], jnp.where(diag, extra, 0.0), jnp.where(mid, extra, 0.0)], 1
    )
    high = parts.astype(BF)
    rest = (parts - f(high)).astype(BF)
    data = spread[0:256] + dot(high, expand_ref[...]) + dot(rest, expand_ref[...])
    packed = pick(chooser, jnp.concatenate([data[:, :KF], data[:, KF:]] + weights, 0))
    sb[...] = packed.reshape(OWNERS, 16, KF)
    rb[cls] = sb[cls]
    used = pl.ds(0, 12)
    went = {
        k: push(sb.at[(cls + k) % OWNERS, used], rb.at[cls, used], owner_at(k)) for k in range(1, OWNERS)
    }
    place = lax.broadcasted_iota(jnp.int32, (KF, OWNERS * 16), 0)
    kind = lax.shift_right_arithmetic(
        lax.broadcasted_iota(jnp.int32, (KF, OWNERS * 16), 1) & 15, 2
    )
    hit = place == cell
    hits = jnp.concatenate(
        [jnp.where(hit & (kind == c), 1.0, 0.0).astype(BF) for c in range(3)], 0
    )
    for k in range(1, OWNERS):
        rb[(cls - k) % OWNERS, 12:16] = jnp.zeros((4, KF), F32)
    for k in range(1, OWNERS):
        take(went[k], rb.at[(cls - k) % OWNERS, used])

    volume = pick(hits, rb[...].reshape(OWNERS * 16, KF))
    scale = 1.0 / (volume[2 * KF :] + 1.0)
    w_re, w_im = volume[:KF] * scale, volume[KF : 2 * KF] * scale
    wz_s[:, 0:KF] = w_re.astype(BF)
    wz_s[:, KF : 2 * KF] = w_im.astype(BF)
    i = push(wz_s, wz_r, twin)

    def collect(q, v):
        for s in range(SHELLS):
            part = jnp.where(shell == s, v, 0.0).reshape(KF // 8, 8, KF)
            bins[q, s * 8 : s * 8 + 8, :] = jnp.sum(part, axis=0)

    collect(1, w_re * w_re + w_im * w_im)
    take(i, wz_r)
    o_re, o_im = f(wz_r[:, 0:KF]), f(wz_r[:, KF : 2 * KF])
    collect(0, w_re * o_re + w_im * o_im)
    collect(2, o_re * o_re + o_im * o_im)
    line = lax.broadcasted_iota(jnp.int32, (8, KF), 0)
    ones = jnp.ones((8, KF), F32)
    group = lax.broadcasted_iota(jnp.int32, (SHELLS * 8, KF), 0) // 8
    group = jnp.where(group == lax.broadcasted_iota(jnp.int32, (SHELLS * 8, KF), 1), 1.0, 0.0)
    sums = jnp.zeros((8, KF), F32)
    for q in range(3):
        part = lax.dot_general(
            ones, bins[q], (((1,), (1,)), ((), ())), precision=lax.Precision.HIGHEST,
            preferred_element_type=F32,
        )
        part = jnp.dot(part, group, precision=lax.Precision.HIGHEST, preferred_element_type=F32)
        sums = jnp.where(line == q, part, sums)
    sz_s[...] = sums
    tags = {j: push(sz_s, sz_r.at[j], at(dz=j)) for j in Z_ORDER[:-1]}
    for j, tag in tags.items():
        take(tag, sz_r.at[j])
        sums = sums + sz_r[j]
    sx_s[...] = sums
    tags = {k: push(sx_s, sx_r.at[k[0], k[1]], device) for k, device in plane_peers.items()}
    for k, tag in tags.items():
        take(tag, sx_r.at[k[0], k[1]])
        sums = sums + sx_r[k[0], k[1]]
    fsc = sums[0:1] / jnp.maximum(jnp.sqrt(sums[1:2] * sums[2:3]), 1.0)
    fsc = jnp.maximum(fsc, 0.0)
    gain = jnp.sqrt(2.0 * fsc / (1.0 + fsc))
    voxel = jnp.zeros((KF, KF), F32)
    for s in range(SHELLS):
        voxel = jnp.where(shell == s, gain[:, s : s + 1], voxel)
    o_ref[0, :, 0:KF] = w_re * voxel
    o_ref[0, :, KF : 2 * KF] = w_im * voxel
    for out in sent:
        out.wait_send()


def left_table():
    table = np.zeros((768, ROWS), np.float32)
    for k in range(CLS_DEV):
        for r in range(KF):
            if r < HK:
                table[k * KF + r, k * HK + r] = 1.0
            elif r > HK:
                table[256 + k * KF + r, k * HK + KF - r] = 1.0
            table[512 + k * KF + r, 2 * HK + k] = 1.0
    return table


def shards(images, references, image_owner, image_class, defocus_bin, slice_cells):
    cos_table, sin_table = dft_tables()
    cs = jnp.asarray(np.concatenate([cos_table, sin_table], 1))
    cst = jnp.asarray(np.concatenate([cos_table.T, sin_table.T], 0))
    both = jnp.asarray(
        np.concatenate(
            [np.concatenate([cos_table, sin_table], 1), np.concatenate([cos_table.T, sin_table.T], 0)], 0
        )
    )
    widen = jnp.asarray(
        np.concatenate(
            [
                np.concatenate([cos_table.T, sin_table.T], 1),
                np.concatenate([-sin_table.T, cos_table.T], 1),
            ],
            0,
        )
    )
    combine = jnp.asarray(np.concatenate([cos_table, -sin_table], 1))
    ctf = jnp.asarray(ctf_table())
    expand = jnp.asarray(expand_tables(), BF)
    turn = jnp.asarray(row_turn(), BF)
    left = jnp.asarray(left_table(), BF)
    local = images.shape[0]
    vmem = pl.BlockSpec(memory_space=pltpu.VMEM)
    anywhere = pl.BlockSpec(memory_space=pltpu.HBM)
    dma = pltpu.SemaphoreType.DMA

    spectra = pl.pallas_call(
        gather_kernel,
        name="gather_references",
        out_shape=jax.ShapeDtypeStruct((NY, NZ, ROWS, 2 * KF), BF),
        in_specs=[anywhere] * 2,
        out_specs=vmem,
        scratch_shapes=[
            pltpu.VMEM((CLS_DEV, PIX, PIX), BF), pltpu.VMEM((2 * PIX, 2 * KF), BF),
            pltpu.VMEM((ROWS, 2 * KF), BF), dma((2,)), dma((GATHER_SEMS,)), dma((GATHER_SEMS,)),
        ],
        compiler_params=pltpu.CompilerParams(
            collective_id=0, has_side_effects=True, vmem_limit_bytes=44 << 20
        ),
    )(references[0], both)

    partial = pl.pallas_call(
        image_kernel,
        name="image_terms",
        out_shape=jax.ShapeDtypeStruct((OWNERS, ROWS, 2 * KF), BF),
        grid_spec=pltpu.PrefetchScalarGridSpec(
            num_scalar_prefetch=3,
            grid=(local // GROUP,),
            in_specs=[
                pl.BlockSpec((GROUP, PIX, PIX), lambda i, *_: (i, 0, 0)),
                *[vmem] * 8,
            ],
            out_specs=vmem,
            scratch_shapes=[pltpu.VMEM((OWNERS, ROWS, 2 * KF), F32)],
        ),
        compiler_params=pltpu.CompilerParams(
            dimension_semantics=("arbitrary",), vmem_limit_bytes=44 << 20
        ),
    )(
        image_owner[:, 0], image_class, defocus_bin, images,
        spectra.reshape(OWNERS, ROWS, 2 * KF), ctf, cs, cst, widen, combine, expand, turn,
    )

    def buf(*shape):
        return pltpu.VMEM(shape, BF)

    wide = 2 * KF
    return pl.pallas_call(
        reduce_kernel,
        name="reduce_maps",
        out_shape=jax.ShapeDtypeStruct((1, KF, 2 * KF), F32),
        in_specs=[vmem] * 3 + [anywhere] * 2,
        out_specs=vmem,
        scratch_shapes=[
            buf(768, 256), buf(768, ROWS), buf(NZ, PA, wide), buf(NZ, PR - PA, wide),
            buf(NZ, PA, wide), buf(NZ, PR - PA, wide), buf(NZ, PR, wide), buf(NZ, PR, wide),
            buf(NZ, PR, wide), buf(NZ, PR, wide),
            pltpu.VMEM((PR, wide), F32), pltpu.VMEM((NX, PR, wide), F32),
            buf(2, NZ, 16, wide), buf(2, NZ, 16, wide), buf(2, NZ, 16, wide), buf(2, NZ, 16, wide),
            buf(NY, NZ, 16, wide), buf(NY, NZ, 16, wide),
            buf(NY, NZ, 16, wide), buf(NY, NZ, 16, wide), buf(NZ, 16, wide), buf(NZ, 16, wide),
            pltpu.VMEM((16, wide), F32), pltpu.VMEM((NX, 16, wide), F32), pltpu.VMEM((ROWS, wide), F32),
            pltpu.VMEM((OWNERS, 16, KF), F32), pltpu.VMEM((OWNERS, 16, KF), F32),
            buf(KF, wide), buf(KF, wide),
            pltpu.VMEM((8, KF), F32), pltpu.VMEM((NZ, 8, KF), F32),
            pltpu.VMEM((8, KF), F32), pltpu.VMEM((NY, NX, 8, KF), F32),
            pltpu.VMEM((3, SHELLS * 8, KF), F32),
            dma((2,)), dma((REDUCE_SEMS,)), dma((REDUCE_SEMS,)),
        ],
        compiler_params=pltpu.CompilerParams(
            collective_id=1, has_side_effects=True, vmem_limit_bytes=40 << 20
        ),
    )(partial.reshape(NY, NZ, ROWS, 2 * KF), ctf, slice_cells, expand, left)


def solution(mesh):
    placed = (
        P(("half", "cls", "tile"), None, None),
        P("half", "cls", None, None),
        P(("half", "cls", "tile"), None),
        P(("half", "cls", "tile")),
        P(("half", "cls", "tile")),
        P(),
    )
    return jax.shard_map(
        shards,
        mesh=mesh,
        in_specs=placed,
        out_specs=P("half", ("cls", "tile"), None),
        check_vma=False,
    )
```

time: 135 us -> 106 us (0.79)
  Pallas kernels: 125 us -> 103 us
  local copies, waits for them, and re-layouts: 7.18 us -> 2.73 us
    pallas_call x1, Pallas kernels: 32.4 us -> 13.6 us  [shards(): pl.pallas_call(image_kernel, name='image_terms', out_shape=jax.ShapeDtype...]
    unnamed x36 -> x29, local copies, waits for them, and re-layouts: 7 us -> 2.73 us
    pallas_call x1, Pallas kernels: 32.7 us -> 29.5 us  [shards(): pl.pallas_call(gather_kernel, name='gather_references', out_shape=jax.Sha...]
where the time goes in v2:
time: 106 us
  Pallas kernels  103 us (97%)
  local copies, waits for them, and re-layouts  2.73 us (3%)
    pallas_call x1, Pallas kernels, shards(): pl.pallas_call(reduce_kernel, name='reduce_maps', out_shape=jax.ShapeDtyp...  60.2 us
    pallas_call x1, Pallas kernels, shards(): pl.pallas_call(gather_kernel, name='gather_references', out_shape=jax.Sha...  29.5 us
    pallas_call x1, Pallas kernels, shards(): pl.pallas_call(image_kernel, name='image_terms', out_shape=jax.ShapeDtype...  13.6 us
    unnamed x29, local copies, waits for them, and re-layouts  2.73 us

profile of v2, /device:TPU:1, one launch (start us, length us, event | category | flops | bytes accessed | tf_op | source)
XLA Modules:
  0.0 106.3 jit_solution(16840240568285348273)
XLA Ops:
  0.0 0.0 copy-start.1
  0.0 0.0 copy-start
  0.0 0.0 copy-start.3
  0.0 0.0 copy-start.4
  0.0 1.1 %copy-done.4 = bf16[1,2,256,256]{3,2,1,0:T(8,128)(2,1)S(1)} copy-done((bf16[1,2,256,256]{3,2,1,0:T(8,128)(2,1)S(1)}, bf16[1,2,256,256]{3,2,1,0:T(8,128)(2,1)}, u32[]{:S(2)}) %copy-start.4) | copy-done | bytes 262168
  1.1 0.0 copy-start.5
  1.1 0.9 copy-done.5
  2.0 0.0 copy-start.6
  2.0 0.0 copy-start.7
  2.0 0.0 copy-start.8
  2.0 0.0 copy-start.10
  2.0 0.0 copy-start.11
  2.1 0.0 copy-start.12
  2.1 0.0 copy-start.13
  2.1 29.5 %gather_references.1 = bf16[4,8,144,256]{3,2,1,0:T(8,128)(2,1)S(1)} custom-call(bf16[2,256,256]{2,1,0:T(8,128)(2,1)S(1)} %bitcast.6, bf16[512,256]{1,0:T(8,128)(2,1)S(1)} %copy-done.5), custom_call_target="tpu_custom_call" | custom-call | tf_op jit(solution)/shard_map/gather_references/pallas_call | solution.py:670
  31.6 0.0 copy-done.1
  31.6 0.0 copy-done
  31.6 0.0 copy-done.3
  31.6 0.0 copy-done.6
  31.6 0.0 copy-done.7
  31.6 0.0 copy-done.8
  31.7 0.0 copy-done.10
  31.7 0.0 copy-done.11
  31.7 0.0 copy-done.12
  31.7 0.0 copy-done.13
  31.7 0.0 copy-start.2
  31.7 0.0 copy-start.9
  31.7 13.6 %image_terms.1 = bf16[32,144,256]{2,1,0:T(8,128)(2,1)S(1)} custom-call(s32[32]{0:T(128)S(1)} %bitcast.7, s32[32]{0:T(128)S(1)} %copy-done.12, s32[32]{0:T(128)S(1)} %copy-done.13, bf16[32,256,256]{2,1,0:T(8,128)(2,1)} %img_ref.1, bf16[32,144,256]{2,1,0:T(8,128)(2,1)S(1)} %bitcast.5, f32[16,128,128]{2,1,0:T(8,128)S(1)} %copy-done, ...), custom_call_target="tpu_custom_call" | custom-call | tf_op jit(solution)/shard_map/image_terms/pallas_call | solution.py:685
  45.4 0.0 copy-done.2
  45.4 0.0 copy-done.9
  45.4 60.2 %reduce_maps.1 = f32[1,128,256]{2,1,0:T(8,128)S(1)} custom-call(bf16[4,8,144,256]{3,2,1,0:T(8,128)(2,1)S(1)} %bitcast.4, f32[16,128,128]{2,1,0:T(8,128)S(1)} %copy-done, s32[64,128]{1,0:T(8,128)S(1)} %copy-done.9, bf16[768,256]{1,0:T(8,128)(2,1)S(1)} %copy-done.1, bf16[768,144]{1,0:T(8,128)(2,1)S(1)} %copy-done.2), custom_call_target="tpu_custom_call" | custom-call | tf_op jit(solution)/shard_map/reduce_maps/pallas_call | solution.py:711
  105.6 0.7 copy.17
Async XLA Ops:
  0.0 31.6 %copy-start.1 = (bf16[768,256]{1,0:T(8,128)(2,1)S(1)}, bf16[768,256]{1,0:T(8,128)(2,1)}, u32[]{:S(2)}) copy-start(bf16[768,256]{1,0:T(8,128)(2,1)} %constant.24.clone.expand_ref.expand_any) | copy-start | bytes 1179652
  0.0 31.6 %copy-start = (f32[16,128,128]{2,1,0:T(8,128)S(1)}, f32[16,128,128]{2,1,0:T(8,128)}, u32[]{:S(2)}) copy-start(f32[16,128,128]{2,1,0:T(8,128)} %constant.23.clone.ctf_ref) | copy-start | bytes 3145732
  0.0 31.6 %copy-start.3 = (bf16[256,512]{1,0:T(8,128)(2,1)S(1)}, bf16[256,512]{1,0:T(8,128)(2,1)}, u32[]{:S(2)}) copy-start(bf16[256,512]{1,0:T(8,128)(2,1)} %constant.21.clone.widen_ref) | copy-start | bytes 786436
  0.0 1.1 %copy-start.4 = (bf16[1,2,256,256]{3,2,1,0:T(8,128)(2,1)S(1)}, bf16[1,2,256,256]{3,2,1,0:T(8,128)(2,1)}, u32[]{:S(2)}) copy-start(bf16[1,2,256,256]{3,2,1,0:T(8,128)(2,1)} %param.16) | copy-start | bytes 786436
  1.1 0.9 copy-start.5
  2.0 29.6 %copy-start.6 = (bf16[256,256]{1,0:T(8,128)(2,1)S(1)}, bf16[256,256]{1,0:T(8,128)(2,1)}, u32[]{:S(2)}) copy-start(bf16[256,256]{1,0:T(8,128)(2,1)} %constant.22.clone.combine_ref) | copy-start | bytes 393220
  2.0 29.6 %copy-start.7 = (bf16[256,256]{1,0:T(8,128)(2,1)S(1)}, bf16[256,256]{1,0:T(8,128)(2,1)}, u32[]{:S(2)}) copy-start(bf16[256,256]{1,0:T(8,128)(2,1)} %constant.19.clone.cst_ref) | copy-start | bytes 393220
  2.0 29.6 %copy-start.8 = (bf16[256,256]{1,0:T(8,128)(2,1)S(1)}, bf16[256,256]{1,0:T(8,128)(2,1)}, u32[]{:S(2)}) copy-start(bf16[256,256]{1,0:T(8,128)(2,1)} %constant.18.clone.cs_ref) | copy-start | bytes 393220
  2.0 29.6 %copy-start.10 = (bf16[64,64]{1,0:T(8,128)(2,1)S(1)}, bf16[64,64]{1,0:T(8,128)(2,1)}, u32[]{:S(2)}) copy-start(bf16[64,64]{1,0:T(8,128)(2,1)} %constant.25.clone.turn_ref) | copy-start | bytes 24580
  2.0 29.6 %copy-start.11 = (s32[32,1]{0,1:T(1,128)S(1)}, s32[32,1]{0,1:T(1,128)}, u32[]{:S(2)}) copy-start(s32[32,1]{0,1:T(1,128)} %param.17) | copy-start | bytes 388
  2.1 29.6 %copy-start.12 = (s32[32]{0:T(128)S(1)}, s32[32]{0:T(128)}, u32[]{:S(2)}) copy-start(s32[32]{0:T(128)} %class_ref.1) | copy-start | bytes 388
  2.1 29.6 %copy-start.13 = (s32[32]{0:T(128)S(1)}, s32[32]{0:T(128)}, u32[]{:S(2)}) copy-start(s32[32]{0:T(128)} %bin_ref.1) | copy-start | bytes 388
  31.7 13.7 %copy-start.2 = (bf16[768,144]{1,0:T(8,128)(2,1)S(1)}, bf16[768,144]{1,0:T(8,128)(2,1)}, u32[]{:S(2)}) copy-start(bf16[768,144]{1,0:T(8,128)(2,1)} %constant.26.clone.left_any) | copy-start | bytes 663556
  31.7 13.7 %copy-start.9 = (s32[64,128]{1,0:T(8,128)S(1)}, s32[64,128]{1,0:T(8,128)}, u32[]{:S(2)}) copy-start(s32[64,128]{1,0:T(8,128)} %cells_ref.1) | copy-start | bytes 98308

commit v3 on v2

--- a/solution.py
+++ b/solution.py
@@ -126,7 +126,10 @@
     barrier = pltpu.get_barrier_semaphore()
     for device in devices:
         pl.semaphore_signal(barrier, inc=1, device_id=device, device_id_type=MESH)
-    pl.semaphore_wait(barrier, len(devices))
+
+
+def greeted(devices):
+    pl.semaphore_wait(pltpu.get_barrier_semaphore(), len(devices))
 
 
 GATHER_SEMS = 80
@@ -142,7 +145,8 @@
     for load in loads:
         load.start()
     _, y, z, tile, at = here()
-    greet([at(dz=k) for k in range(1, NZ)] + [at(dy=1), at(dy=-1), at(dx=1), at(dx=-1)])
+    friends = [at(dz=k) for k in range(1, NZ)] + [at(dy=1), at(dy=-1), at(dx=1), at(dx=-1)]
+    greet(friends)
     for load in loads:
         load.wait()
     line = lax.broadcasted_iota(jnp.int32, (16, KF), 0)
@@ -186,6 +190,7 @@
     east, west = at(dx=1), at(dx=-1)
     yw, ye, yo = (y - 1) % NY, (y + 1) % NY, (y + 2) % NY
 
+    greeted(friends)
     r_tags = {j: push((y, z, mine), at(dz=j)) for j in (4, 3, 5, 2, 6, 1, 7)}
     p_up, p_down = push((y, z, whole), up), push((y, z, whole), down)
     waiting, last = [], []
@@ -397,11 +402,21 @@
     plane_peers = {
         (dy, dx): at(dy=dy, dx=dx) for dy in (2, 1, 3, 0) for dx in (2, 1, 3, 0) if dy or dx
     }
-    greet(
-        [owner_at(k) for k in range(1, OWNERS)]
-        + [device for (dy, dx), device in plane_peers.items() if dx]
-        + [twin]
-    )
+    friends = [at(dz=k) for k in range(1, NZ)] + [north, south, at(dy=2), east, west, at(dx=2), twin]
+    greet(friends)
+    slot, cell = routes(cells_ref[...], cls, tile)
+    place = lax.broadcasted_iota(jnp.int32, (OWNERS * 16, 2 * KF), 0)
+    chooser = jnp.concatenate(
+        [jnp.where(place == slot + 4 * c, 1.0, 0.0).astype(BF) for c in range(3)], 1
+    )
+    d0 = lax.broadcasted_iota(jnp.int32, (KF, KF), 0) - HK
+    d1 = lax.broadcasted_iota(jnp.int32, (KF, KF), 1) - HK
+    plane = cls * NX + tile - HK
+    radius = plane * plane + d0 * d0 + d1 * d1
+    shell = jnp.zeros((KF, KF), jnp.int32)
+    for s in range(1, SHELLS):
+        shell = jnp.where(radius >= s * s, s, shell)
+    greeted(friends)
     sent = []
 
     def push(src, dst, device):
@@ -436,36 +451,23 @@
             push(d_ref.at[yo, zz, back], pin_m.at[j], south),
         )
     plain_p, plain_r = {}, {}
-    for n, j in enumerate(Z_ORDER):
+    for n in range(NY):
+        if n < 2:
+            plain_r[n] = push(d_ref.at[n, every, along(-1)], rr_m.at[n], west)
+        else:
+            plain_r[n] = push(d_ref.at[n, every, along(1)], rr_p.at[n], east)
+
+    def plain(j):
         zz = (z + j) % NZ
-        if n < NY:
-            if n < 2:
-                plain_r[n] = push(d_ref.at[n, every, along(-1)], rr_m.at[n], west)
-            else:
-                plain_r[n] = push(d_ref.at[n, every, along(1)], rr_p.at[n], east)
         plain_p[j] = (
             push(d_ref.at[yn, zz, back], pr_p.at[j, back], north),
             push(d_ref.at[ys, zz, front], pr_m.at[j, front], south),
         )
 
-    slot, cell = routes(cells_ref[...], cls, tile)
-    place = lax.broadcasted_iota(jnp.int32, (OWNERS * 16, 2 * KF), 0)
-    chooser = jnp.concatenate(
-        [jnp.where(place == slot + 4 * c, 1.0, 0.0).astype(BF) for c in range(3)], 1
-    )
-
-    second_p, second_r = {}, {}
-    for n, j in enumerate(Z_ORDER):
+    second_p, second_r, third_p = {}, {}, {}
+
+    def relay(j):
         zz = (z + j) % NZ
-        if n < NY:
-            if n < 2:
-                take(first_r[n], rin_p.at[n])
-                rs_p[n] = (f(d_ref[n, every, along(1)]) + f(rin_p[n])).astype(BF)
-                second_r[n] = push(rs_p.at[n], rr_p.at[n], east)
-            else:
-                take(first_r[n], rin_m.at[n - 2])
-                rs_m[n - 2] = (f(d_ref[n, every, along(-1)]) + f(rin_m[n - 2])).astype(BF)
-                second_r[n] = push(rs_m.at[n - 2], rr_m.at[n], west)
         a, b = first_p[j]
         take(a, pin_p.at[j])
         ps_p[j] = (f(d_ref[yn, zz, front]) + f(pin_p[j])).astype(BF)
@@ -475,7 +477,15 @@
         b = push(ps_m.at[j], pr_m.at[j, back], south)
         second_p[j] = a, b
 
-    third_p = {}
+    def relay_r(n):
+        if n < 2:
+            take(first_r[n], rin_p.at[n])
+            rs_p[n] = (f(d_ref[n, every, along(1)]) + f(rin_p[n])).astype(BF)
+            second_r[n] = push(rs_p.at[n], rr_p.at[n], east)
+        else:
+            take(first_r[n], rin_m.at[n - 2])
+            rs_m[n - 2] = (f(d_ref[n, every, along(-1)]) + f(rin_m[n - 2])).astype(BF)
+            second_r[n] = push(rs_m.at[n - 2], rr_m.at[n], west)
 
     def settle(j):
         zz = (z + j) % NZ
@@ -489,30 +499,35 @@
         if j:
             third_p[j] = push(pz_s.at[j], pz_r.at[j], at(dz=j))
 
-    for n, j in enumerate(Z_ORDER[:4]):
-        settle(j)
+    def settle_r(n):
         take(second_r[n], (rr_p if n < 2 else rr_m).at[n])
         take(plain_r[n], (rr_m if n < 2 else rr_p).at[n])
         ry_s[n] = (f(d_ref[n, every, along(0)]) + f(rr_p[n]) + f(rr_m[n])).astype(BF)
-    third_r = {k: push(ry_s.at[(y + k) % NY], ry_r.at[k], at(dy=k)) for k in (2, 1, 3)}
-    for j in Z_ORDER[4:6]:
-        settle(j)
-    total = f(ry_s[y])
-    for k in (1, 2, 3):
-        take(third_r[k], ry_r.at[k])
-        total = total + f(ry_r[k])
-    rz_s[...] = total.astype(BF)
-    fourth_r = {j: push(rz_s.at[(z + j) % NZ], rz_r.at[j], at(dz=j)) for j in Z_ORDER[:-1]}
-    for j in Z_ORDER[6:]:
-        settle(j)
-
-    d0 = lax.broadcasted_iota(jnp.int32, (KF, KF), 0) - HK
-    d1 = lax.broadcasted_iota(jnp.int32, (KF, KF), 1) - HK
-    plane = cls * NX + tile - HK
-    radius = plane * plane + d0 * d0 + d1 * d1
-    shell = jnp.zeros((KF, KF), jnp.int32)
-    for s in range(1, SHELLS):
-        shell = jnp.where(radius >= s * s, s, shell)
+
+    for j in Z_ORDER[:3]:
+        plain(j)
+    for n in range(NZ + 3):
+        if n < NZ:
+            if n < NY:
+                relay_r(n)
+            relay(Z_ORDER[n])
+            if n + 3 < NZ:
+                plain(Z_ORDER[n + 3])
+        if n >= 3:
+            if n < 3 + NY:
+                settle_r(n - 3)
+            settle(Z_ORDER[n - 3])
+        if n == 2 + NY:
+            third_r = {k: push(ry_s.at[(y + k) % NY], ry_r.at[k], at(dy=k)) for k in (2, 1, 3)}
+        if n == 4 + NY:
+            total = f(ry_s[y])
+            for k in (1, 2, 3):
+                take(third_r[k], ry_r.at[k])
+                total = total + f(ry_r[k])
+            rz_s[...] = total.astype(BF)
+            fourth_r = {
+                j: push(rz_s.at[(z + j) % NZ], rz_r.at[j], at(dz=j)) for j in Z_ORDER[:-1]
+            }
 
     total = f(rz_s[z])
     for j in range(1, NZ):
@@ -582,29 +597,30 @@
     wz_s[:, 0:KF] = w_re.astype(BF)
     wz_s[:, KF : 2 * KF] = w_im.astype(BF)
     i = push(wz_s, wz_r, twin)
+    bins[3 * SHELLS :, :] = jnp.zeros((SHELLS, KF), F32)
 
     def collect(q, v):
         for s in range(SHELLS):
-            part = jnp.where(shell == s, v, 0.0).reshape(KF // 8, 8, KF)
-            bins[q, s * 8 : s * 8 + 8, :] = jnp.sum(part, axis=0)
+            part = jnp.sum(jnp.where(shell == s, v, 0.0), axis=0, keepdims=True)
+            bins[q * SHELLS + s : q * SHELLS + s + 1, :] = part
 
     collect(1, w_re * w_re + w_im * w_im)
     take(i, wz_r)
     o_re, o_im = f(wz_r[:, 0:KF]), f(wz_r[:, KF : 2 * KF])
     collect(0, w_re * o_re + w_im * o_im)
     collect(2, o_re * o_re + o_im * o_im)
-    line = lax.broadcasted_iota(jnp.int32, (8, KF), 0)
-    ones = jnp.ones((8, KF), F32)
-    group = lax.broadcasted_iota(jnp.int32, (SHELLS * 8, KF), 0) // 8
-    group = jnp.where(group == lax.broadcasted_iota(jnp.int32, (SHELLS * 8, KF), 1), 1.0, 0.0)
-    sums = jnp.zeros((8, KF), F32)
-    for q in range(3):
-        part = lax.dot_general(
-            ones, bins[q], (((1,), (1,)), ((), ())), precision=lax.Precision.HIGHEST,
-            preferred_element_type=F32,
+
+    def across(v):
+        return lax.dot_general(
+            jnp.ones((8, KF), BF), v, (((1,), (1,)), ((), ())), preferred_element_type=F32
         )
-        part = jnp.dot(part, group, precision=lax.Precision.HIGHEST, preferred_element_type=F32)
-        sums = jnp.where(line == q, part, sums)
+
+    rest = bins[...]
+    sums = jnp.zeros((8, 4 * SHELLS), F32)
+    for _ in range(3):
+        high = rest.astype(BF)
+        sums = sums + across(high)
+        rest = rest - f(high)
     sz_s[...] = sums
     tags = {j: push(sz_s, sz_r.at[j], at(dz=j)) for j in Z_ORDER[:-1]}
     for j, tag in tags.items():
@@ -615,7 +631,8 @@
     for k, tag in tags.items():
         take(tag, sx_r.at[k[0], k[1]])
         sums = sums + sx_r[k[0], k[1]]
-    fsc = sums[0:1] / jnp.maximum(jnp.sqrt(sums[1:2] * sums[2:3]), 1.0)
+    sums = [sums[0:1, q * SHELLS : (q + 1) * SHELLS] for q in range(3)]
+    fsc = sums[0] / jnp.maximum(jnp.sqrt(sums[1] * sums[2]), 1.0)
     fsc = jnp.maximum(fsc, 0.0)
     gain = jnp.sqrt(2.0 * fsc / (1.0 + fsc))
     voxel = jnp.zeros((KF, KF), F32)
@@ -725,9 +742,9 @@
             pltpu.VMEM((16, wide), F32), pltpu.VMEM((NX, 16, wide), F32), pltpu.VMEM((ROWS, wide), F32),
             pltpu.VMEM((OWNERS, 16, KF), F32), pltpu.VMEM((OWNERS, 16, KF), F32),
             buf(KF, wide), buf(KF, wide),
-            pltpu.VMEM((8, KF), F32), pltpu.VMEM((NZ, 8, KF), F32),
-            pltpu.VMEM((8, KF), F32), pltpu.VMEM((NY, NX, 8, KF), F32),
-            pltpu.VMEM((3, SHELLS * 8, KF), F32),
+            pltpu.VMEM((8, 4 * SHELLS), F32), pltpu.VMEM((NZ, 8, 4 * SHELLS), F32),
+            pltpu.VMEM((8, 4 * SHELLS), F32), pltpu.VMEM((NY, NX, 8, 4 * SHELLS), F32),
+            pltpu.VMEM((4 * SHELLS, KF), F32),
             dma((2,)), dma((REDUCE_SEMS,)), dma((REDUCE_SEMS,)),
         ],
         compiler_params=pltpu.CompilerParams(

time: 106 us -> 104 us (0.981)
  Pallas kernels: 103 us -> 101 us
    pallas_call x1, Pallas kernels: 60.2 us -> 58.7 us  [shards(): pl.pallas_call(reduce_kernel, name='reduce_maps', out_shape=jax.ShapeDtyp...]
where the time goes in v3:
time: 104 us
  Pallas kernels  101 us (97%)
  local copies, waits for them, and re-layouts  2.73 us (3%)
    pallas_call x1, Pallas kernels, shards(): pl.pallas_call(reduce_kernel, name='reduce_maps', out_shape=jax.ShapeDtyp...  58.7 us
    pallas_call x1, Pallas kernels, shards(): pl.pallas_call(gather_kernel, name='gather_references', out_shape=jax.Sha...  28.9 us
    pallas_call x1, Pallas kernels, shards(): pl.pallas_call(image_kernel, name='image_terms', out_shape=jax.ShapeDtype...  13.6 us
    unnamed x29, local copies, waits for them, and re-layouts  2.73 us

profile of v3, /device:TPU:1, one launch (start us, length us, event | category | flops | bytes accessed | tf_op | source)
XLA Modules:
  0.0 104.2 jit_solution(12517476597494356729)
XLA Ops:
  0.0 0.0 copy-start.1
  0.0 0.0 copy-start
  0.0 0.0 copy-start.3
  0.0 0.0 copy-start.4
  0.0 1.1 %copy-done.4 = bf16[1,2,256,256]{3,2,1,0:T(8,128)(2,1)S(1)} copy-done((bf16[1,2,256,256]{3,2,1,0:T(8,128)(2,1)S(1)}, bf16[1,2,256,256]{3,2,1,0:T(8,128)(2,1)}, u32[]{:S(2)}) %copy-start.4) | copy-done | bytes 262168
  1.1 0.0 copy-start.5
  1.1 0.9 copy-done.5
  2.0 0.0 copy-start.6
  2.0 0.0 copy-start.7
  2.0 0.0 copy-start.8
  2.0 0.0 copy-start.10
  2.0 0.0 copy-start.11
  2.1 0.0 copy-start.12
  2.1 0.0 copy-start.13
  2.1 28.9 %gather_references.1 = bf16[4,8,144,256]{3,2,1,0:T(8,128)(2,1)S(1)} custom-call(bf16[2,256,256]{2,1,0:T(8,128)(2,1)S(1)} %bitcast.6, bf16[512,256]{1,0:T(8,128)(2,1)S(1)} %copy-done.5), custom_call_target="tpu_custom_call" | custom-call | tf_op jit(solution)/shard_map/gather_references/pallas_call | solution.py:687
  31.0 0.0 copy-done.1
  31.0 0.0 copy-done
  31.1 0.0 copy-done.3
  31.1 0.0 copy-done.6
  31.1 0.0 copy-done.7
  31.1 0.0 copy-done.8
  31.1 0.0 copy-done.10
  31.1 0.0 copy-done.11
  31.1 0.0 copy-done.12
  31.1 0.0 copy-done.13
  31.1 0.0 copy-start.2
  31.1 0.0 copy-start.9
  31.2 13.6 %image_terms.1 = bf16[32,144,256]{2,1,0:T(8,128)(2,1)S(1)} custom-call(s32[32]{0:T(128)S(1)} %bitcast.7, s32[32]{0:T(128)S(1)} %copy-done.12, s32[32]{0:T(128)S(1)} %copy-done.13, bf16[32,256,256]{2,1,0:T(8,128)(2,1)} %img_ref.1, bf16[32,144,256]{2,1,0:T(8,128)(2,1)S(1)} %bitcast.5, f32[16,128,128]{2,1,0:T(8,128)S(1)} %copy-done, ...), custom_call_target="tpu_custom_call" | custom-call | tf_op jit(solution)/shard_map/image_terms/pallas_call | solution.py:702
  44.8 0.0 copy-done.2
  44.8 0.0 copy-done.9
  44.8 58.7 %reduce_maps.1 = f32[1,128,256]{2,1,0:T(8,128)S(1)} custom-call(bf16[4,8,144,256]{3,2,1,0:T(8,128)(2,1)S(1)} %bitcast.4, f32[16,128,128]{2,1,0:T(8,128)S(1)} %copy-done, s32[64,128]{1,0:T(8,128)S(1)} %copy-done.9, bf16[768,256]{1,0:T(8,128)(2,1)S(1)} %copy-done.1, bf16[768,144]{1,0:T(8,128)(2,1)S(1)} %copy-done.2), custom_call_target="tpu_custom_call" | custom-call | tf_op jit(solution)/shard_map/reduce_maps/pallas_call | solution.py:728
  103.6 0.7 copy.17
Async XLA Ops:
  0.0 31.0 %copy-start.1 = (bf16[768,256]{1,0:T(8,128)(2,1)S(1)}, bf16[768,256]{1,0:T(8,128)(2,1)}, u32[]{:S(2)}) copy-start(bf16[768,256]{1,0:T(8,128)(2,1)} %constant.24.clone.expand_ref.expand_any) | copy-start | bytes 1179652
  0.0 31.0 %copy-start = (f32[16,128,128]{2,1,0:T(8,128)S(1)}, f32[16,128,128]{2,1,0:T(8,128)}, u32[]{:S(2)}) copy-start(f32[16,128,128]{2,1,0:T(8,128)} %constant.23.clone.ctf_ref) | copy-start | bytes 3145732
  0.0 31.0 %copy-start.3 = (bf16[256,512]{1,0:T(8,128)(2,1)S(1)}, bf16[256,512]{1,0:T(8,128)(2,1)}, u32[]{:S(2)}) copy-start(bf16[256,512]{1,0:T(8,128)(2,1)} %constant.21.clone.widen_ref) | copy-start | bytes 786436
  0.0 1.1 %copy-start.4 = (bf16[1,2,256,256]{3,2,1,0:T(8,128)(2,1)S(1)}, bf16[1,2,256,256]{3,2,1,0:T(8,128)(2,1)}, u32[]{:S(2)}) copy-start(bf16[1,2,256,256]{3,2,1,0:T(8,128)(2,1)} %param.16) | copy-start | bytes 786436
  1.1 0.9 copy-start.5
  2.0 29.0 %copy-start.6 = (bf16[256,256]{1,0:T(8,128)(2,1)S(1)}, bf16[256,256]{1,0:T(8,128)(2,1)}, u32[]{:S(2)}) copy-start(bf16[256,256]{1,0:T(8,128)(2,1)} %constant.22.clone.combine_ref) | copy-start | bytes 393220
  2.0 29.0 %copy-start.7 = (bf16[256,256]{1,0:T(8,128)(2,1)S(1)}, bf16[256,256]{1,0:T(8,128)(2,1)}, u32[]{:S(2)}) copy-start(bf16[256,256]{1,0:T(8,128)(2,1)} %constant.19.clone.cst_ref) | copy-start | bytes 393220
  2.0 29.0 %copy-start.8 = (bf16[256,256]{1,0:T(8,128)(2,1)S(1)}, bf16[256,256]{1,0:T(8,128)(2,1)}, u32[]{:S(2)}) copy-start(bf16[256,256]{1,0:T(8,128)(2,1)} %constant.18.clone.cs_ref) | copy-start | bytes 393220
  2.0 29.1 %copy-start.10 = (bf16[64,64]{1,0:T(8,128)(2,1)S(1)}, bf16[64,64]{1,0:T(8,128)(2,1)}, u32[]{:S(2)}) copy-start(bf16[64,64]{1,0:T(8,128)(2,1)} %constant.25.clone.turn_ref) | copy-start | bytes 24580
  2.0 29.1 %copy-start.11 = (s32[32,1]{0,1:T(1,128)S(1)}, s32[32,1]{0,1:T(1,128)}, u32[]{:S(2)}) copy-start(s32[32,1]{0,1:T(1,128)} %param.17) | copy-start | bytes 388
  2.1 29.1 %copy-start.12 = (s32[32]{0:T(128)S(1)}, s32[32]{0:T(128)}, u32[]{:S(2)}) copy-start(s32[32]{0:T(128)} %class_ref.1) | copy-start | bytes 388
  2.1 29.1 %copy-start.13 = (s32[32]{0:T(128)S(1)}, s32[32]{0:T(128)}, u32[]{:S(2)}) copy-start(s32[32]{0:T(128)} %bin_ref.1) | copy-start | bytes 388
  31.1 13.7 %copy-start.2 = (bf16[768,144]{1,0:T(8,128)(2,1)S(1)}, bf16[768,144]{1,0:T(8,128)(2,1)}, u32[]{:S(2)}) copy-start(bf16[768,144]{1,0:T(8,128)(2,1)} %constant.26.clone.left_any) | copy-start | bytes 663556
  31.1 13.7 %copy-start.9 = (s32[64,128]{1,0:T(8,128)S(1)}, s32[64,128]{1,0:T(8,128)}, u32[]{:S(2)}) copy-start(s32[64,128]{1,0:T(8,128)} %cells_ref.1) | copy-start | bytes 98308

commit v4 on v3

--- a/solution.py
+++ b/solution.py
@@ -382,7 +382,7 @@
     expand_ref, left_ref, pin_p, pin_m, ps_p, ps_m, pr_p, pr_m, pz_s, pz_r, px_s, px_r,
     rin_p, rin_m, rs_p, rs_m, rr_p, rr_m, ry_s, ry_r, rz_s, rz_r, rx_s, rx_r,
     held, sb, rb, wz_s, wz_r, sz_s, sz_r, sx_s, sx_r, bins,
-    copy_sem, send_sem, recv_sem,
+    copy_sem, far_send, far_recv, send_sem, recv_sem,
 ):
     half, y, z, tile, at = here()
     cls = y * NZ + z
@@ -414,8 +414,8 @@
     plane = cls * NX + tile - HK
     radius = plane * plane + d0 * d0 + d1 * d1
     shell = jnp.zeros((KF, KF), jnp.int32)
-    for s in range(1, SHELLS):
-        shell = jnp.where(radius >= s * s, s, shell)
+    shell = lax.fori_loop(1, SHELLS, lambda s, v: jnp.where(radius >= s * s, s, v), shell)
+    rb[:, 12:16, :] = jnp.zeros((OWNERS, 4, KF), F32)
     greeted(friends)
     sent = []
 
@@ -575,9 +575,26 @@
     sb[...] = packed.reshape(OWNERS, 16, KF)
     rb[cls] = sb[cls]
     used = pl.ds(0, 12)
-    went = {
-        k: push(sb.at[(cls + k) % OWNERS, used], rb.at[cls, used], owner_at(k)) for k in range(1, OWNERS)
-    }
+
+    def scatter(k):
+        return remote(
+            sb.at[(cls + k) % OWNERS, used], rb.at[cls, used], far_send.at[k], far_recv.at[k], owner_at(k)
+        )
+
+    def start(k, carry):
+        scatter(k).start()
+        return carry
+
+    def arrive(k, carry):
+        rows = rb.at[(cls + OWNERS - k) % OWNERS, used]
+        remote(rows, rows, far_send.at[k], far_recv.at[k], owner_at(k)).wait_recv()
+        return carry
+
+    def leave(k, carry):
+        scatter(k).wait_send()
+        return carry
+
+    lax.fori_loop(1, OWNERS, start, 0)
     place = lax.broadcasted_iota(jnp.int32, (KF, OWNERS * 16), 0)
     kind = lax.shift_right_arithmetic(
         lax.broadcasted_iota(jnp.int32, (KF, OWNERS * 16), 1) & 15, 2
@@ -586,10 +603,7 @@
     hits = jnp.concatenate(
         [jnp.where(hit & (kind == c), 1.0, 0.0).astype(BF) for c in range(3)], 0
     )
-    for k in range(1, OWNERS):
-        rb[(cls - k) % OWNERS, 12:16] = jnp.zeros((4, KF), F32)
-    for k in range(1, OWNERS):
-        take(went[k], rb.at[(cls - k) % OWNERS, used])
+    lax.fori_loop(1, OWNERS, arrive, 0)
 
     volume = pick(hits, rb[...].reshape(OWNERS * 16, KF))
     scale = 1.0 / (volume[2 * KF :] + 1.0)
@@ -599,16 +613,22 @@
     i = push(wz_s, wz_r, twin)
     bins[3 * SHELLS :, :] = jnp.zeros((SHELLS, KF), F32)
 
-    def collect(q, v):
-        for s in range(SHELLS):
-            part = jnp.sum(jnp.where(shell == s, v, 0.0), axis=0, keepdims=True)
-            bins[q * SHELLS + s : q * SHELLS + s + 1, :] = part
-
-    collect(1, w_re * w_re + w_im * w_im)
+    def collect(parts):
+        def some(t, carry):
+            for q, v in parts.items():
+                lines = [
+                    jnp.sum(jnp.where(shell == t * 8 + n, v, 0.0), axis=0, keepdims=True)
+                    for n in range(8)
+                ]
+                bins[pl.ds(pl.multiple_of(q * SHELLS + t * 8, 8), 8), :] = jnp.concatenate(lines, 0)
+            return carry
+
+        lax.fori_loop(0, SHELLS // 8, some, 0)
+
+    collect({1: w_re * w_re + w_im * w_im})
     take(i, wz_r)
     o_re, o_im = f(wz_r[:, 0:KF]), f(wz_r[:, KF : 2 * KF])
-    collect(0, w_re * o_re + w_im * o_im)
-    collect(2, o_re * o_re + o_im * o_im)
+    collect({0: w_re * o_re + w_im * o_im, 2: o_re * o_re + o_im * o_im})
 
     def across(v):
         return lax.dot_general(
@@ -640,6 +660,7 @@
         voxel = jnp.where(shell == s, gain[:, s : s + 1], voxel)
     o_ref[0, :, 0:KF] = w_re * voxel
     o_ref[0, :, KF : 2 * KF] = w_im * voxel
+    lax.fori_loop(1, OWNERS, leave, 0)
     for out in sent:
         out.wait_send()
 
@@ -745,7 +766,7 @@
             pltpu.VMEM((8, 4 * SHELLS), F32), pltpu.VMEM((NZ, 8, 4 * SHELLS), F32),
             pltpu.VMEM((8, 4 * SHELLS), F32), pltpu.VMEM((NY, NX, 8, 4 * SHELLS), F32),
             pltpu.VMEM((4 * SHELLS, KF), F32),
-            dma((2,)), dma((REDUCE_SEMS,)), dma((REDUCE_SEMS,)),
+            dma((2,)), dma((OWNERS,)), dma((OWNERS,)), dma((REDUCE_SEMS,)), dma((REDUCE_SEMS,)),
         ],
         compiler_params=pltpu.CompilerParams(
             collective_id=1, has_side_effects=True, vmem_limit_bytes=40 << 20

time: 104 us -> 105 us (level)
  no operation moved by 1% of the time
where the time goes in v4:
time: 105 us
  Pallas kernels  102 us (97%)
  local copies, waits for them, and re-layouts  2.73 us (3%)
    pallas_call x1, Pallas kernels, shards(): pl.pallas_call(reduce_kernel, name='reduce_maps', out_shape=jax.ShapeDtyp...  59.7 us
    pallas_call x1, Pallas kernels, shards(): pl.pallas_call(gather_kernel, name='gather_references', out_shape=jax.Sha...  28.9 us
    pallas_call x1, Pallas kernels, shards(): pl.pallas_call(image_kernel, name='image_terms', out_shape=jax.ShapeDtype...  13.6 us
    unnamed x29, local copies, waits for them, and re-layouts  2.73 us

profile of v4, /device:TPU:1, one launch (start us, length us, event | category | flops | bytes accessed | tf_op | source)
XLA Modules:
  0.0 105.2 jit_solution(8269438567797530777)
XLA Ops:
  0.0 0.0 copy-start.1
  0.0 0.0 copy-start
  0.0 0.0 copy-start.3
  0.0 0.0 copy-start.4
  0.0 1.1 %copy-done.4 = bf16[1,2,256,256]{3,2,1,0:T(8,128)(2,1)S(1)} copy-done((bf16[1,2,256,256]{3,2,1,0:T(8,128)(2,1)S(1)}, bf16[1,2,256,256]{3,2,1,0:T(8,128)(2,1)}, u32[]{:S(2)}) %copy-start.4) | copy-done | bytes 262168
  1.1 0.0 copy-start.5
  1.1 0.9 copy-done.5
  2.0 0.0 copy-start.6
  2.0 0.0 copy-start.7
  2.0 0.0 copy-start.8
  2.0 0.0 copy-start.10
  2.0 0.0 copy-start.11
  2.1 0.0 copy-start.12
  2.1 0.0 copy-start.13
  2.1 28.9 %gather_references.1 = bf16[4,8,144,256]{3,2,1,0:T(8,128)(2,1)S(1)} custom-call(bf16[2,256,256]{2,1,0:T(8,128)(2,1)S(1)} %bitcast.6, bf16[512,256]{1,0:T(8,128)(2,1)S(1)} %copy-done.5), custom_call_target="tpu_custom_call" | custom-call | tf_op jit(solution)/shard_map/gather_references/pallas_call | solution.py:708
  31.0 0.0 copy-done.1
  31.0 0.0 copy-done
  31.1 0.0 copy-done.3
  31.1 0.0 copy-done.6
  31.1 0.0 copy-done.7
  31.1 0.0 copy-done.8
  31.1 0.0 copy-done.10
  31.1 0.0 copy-done.11
  31.1 0.0 copy-done.12
  31.1 0.0 copy-done.13
  31.1 0.0 copy-start.2
  31.1 0.0 copy-start.9
  31.2 13.6 %image_terms.1 = bf16[32,144,256]{2,1,0:T(8,128)(2,1)S(1)} custom-call(s32[32]{0:T(128)S(1)} %bitcast.7, s32[32]{0:T(128)S(1)} %copy-done.12, s32[32]{0:T(128)S(1)} %copy-done.13, bf16[32,256,256]{2,1,0:T(8,128)(2,1)} %img_ref.1, bf16[32,144,256]{2,1,0:T(8,128)(2,1)S(1)} %bitcast.5, f32[16,128,128]{2,1,0:T(8,128)S(1)} %copy-done, ...), custom_call_target="tpu_custom_call" | custom-call | tf_op jit(solution)/shard_map/image_terms/pallas_call | solution.py:723
  44.8 0.0 copy-done.2
  44.8 0.0 copy-done.9
  44.8 59.7 %reduce_maps.1 = f32[1,128,256]{2,1,0:T(8,128)S(1)} custom-call(bf16[4,8,144,256]{3,2,1,0:T(8,128)(2,1)S(1)} %bitcast.4, f32[16,128,128]{2,1,0:T(8,128)S(1)} %copy-done, s32[64,128]{1,0:T(8,128)S(1)} %copy-done.9, bf16[768,256]{1,0:T(8,128)(2,1)S(1)} %copy-done.1, bf16[768,144]{1,0:T(8,128)(2,1)S(1)} %copy-done.2), custom_call_target="tpu_custom_call" | custom-call | tf_op jit(solution)/shard_map/reduce_maps/pallas_call | solution.py:749
  104.6 0.7 copy.17
Async XLA Ops:
  0.0 31.0 %copy-start.1 = (bf16[768,256]{1,0:T(8,128)(2,1)S(1)}, bf16[768,256]{1,0:T(8,128)(2,1)}, u32[]{:S(2)}) copy-start(bf16[768,256]{1,0:T(8,128)(2,1)} %constant.24.clone.expand_ref.expand_any) | copy-start | bytes 1179652
  0.0 31.0 %copy-start = (f32[16,128,128]{2,1,0:T(8,128)S(1)}, f32[16,128,128]{2,1,0:T(8,128)}, u32[]{:S(2)}) copy-start(f32[16,128,128]{2,1,0:T(8,128)} %constant.23.clone.ctf_ref) | copy-start | bytes 3145732
  0.0 31.0 %copy-start.3 = (bf16[256,512]{1,0:T(8,128)(2,1)S(1)}, bf16[256,512]{1,0:T(8,128)(2,1)}, u32[]{:S(2)}) copy-start(bf16[256,512]{1,0:T(8,128)(2,1)} %constant.21.clone.widen_ref) | copy-start | bytes 786436
  0.0 1.1 %copy-start.4 = (bf16[1,2,256,256]{3,2,1,0:T(8,128)(2,1)S(1)}, bf16[1,2,256,256]{3,2,1,0:T(8,128)(2,1)}, u32[]{:S(2)}) copy-start(bf16[1,2,256,256]{3,2,1,0:T(8,128)(2,1)} %param.16) | copy-start | bytes 786436
  1.1 0.9 copy-start.5
  2.0 29.0 %copy-start.6 = (bf16[256,256]{1,0:T(8,128)(2,1)S(1)}, bf16[256,256]{1,0:T(8,128)(2,1)}, u32[]{:S(2)}) copy-start(bf16[256,256]{1,0:T(8,128)(2,1)} %constant.22.clone.combine_ref) | copy-start | bytes 393220
  2.0 29.0 %copy-start.7 = (bf16[256,256]{1,0:T(8,128)(2,1)S(1)}, bf16[256,256]{1,0:T(8,128)(2,1)}, u32[]{:S(2)}) copy-start(bf16[256,256]{1,0:T(8,128)(2,1)} %constant.19.clone.cst_ref) | copy-start | bytes 393220
  2.0 29.0 %copy-start.8 = (bf16[256,256]{1,0:T(8,128)(2,1)S(1)}, bf16[256,256]{1,0:T(8,128)(2,1)}, u32[]{:S(2)}) copy-start(bf16[256,256]{1,0:T(8,128)(2,1)} %constant.18.clone.cs_ref) | copy-start | bytes 393220
  2.0 29.1 %copy-start.10 = (bf16[64,64]{1,0:T(8,128)(2,1)S(1)}, bf16[64,64]{1,0:T(8,128)(2,1)}, u32[]{:S(2)}) copy-start(bf16[64,64]{1,0:T(8,128)(2,1)} %constant.25.clone.turn_ref) | copy-start | bytes 24580
  2.0 29.1 %copy-start.11 = (s32[32,1]{0,1:T(1,128)S(1)}, s32[32,1]{0,1:T(1,128)}, u32[]{:S(2)}) copy-start(s32[32,1]{0,1:T(1,128)} %param.17) | copy-start | bytes 388
  2.1 29.1 %copy-start.12 = (s32[32]{0:T(128)S(1)}, s32[32]{0:T(128)}, u32[]{:S(2)}) copy-start(s32[32]{0:T(128)} %class_ref.1) | copy-start | bytes 388
  2.1 29.1 %copy-start.13 = (s32[32]{0:T(128)S(1)}, s32[32]{0:T(128)}, u32[]{:S(2)}) copy-start(s32[32]{0:T(128)} %bin_ref.1) | copy-start | bytes 388
  31.1 13.7 %copy-start.2 = (bf16[768,144]{1,0:T(8,128)(2,1)S(1)}, bf16[768,144]{1,0:T(8,128)(2,1)}, u32[]{:S(2)}) copy-start(bf16[768,144]{1,0:T(8,128)(2,1)} %constant.26.clone.left_any) | copy-start | bytes 663556
  31.1 13.7 %copy-start.9 = (s32[64,128]{1,0:T(8,128)S(1)}, s32[64,128]{1,0:T(8,128)}, u32[]{:S(2)}) copy-start(s32[64,128]{1,0:T(8,128)} %cells_ref.1) | copy-start | bytes 98308

commit v5 on v3

--- a/solution.py
+++ b/solution.py
@@ -20,7 +20,7 @@
 ROWS = 144
 PR = 80
 PA = 48
-GROUP = 8
+GROUP = 16
 
 sharpness = 40.0
 ctf_scale = 6.0

time: 104 us -> 104 us (level)
  no operation moved by 1% of the time
where the time goes in v5:
time: 104 us
  Pallas kernels  101 us (97%)
  local copies, waits for them, and re-layouts  2.73 us (3%)
    pallas_call x1, Pallas kernels, shards(): pl.pallas_call(reduce_kernel, name='reduce_maps', out_shape=jax.ShapeDtyp...  58.8 us
    pallas_call x1, Pallas kernels, shards(): pl.pallas_call(gather_kernel, name='gather_references', out_shape=jax.Sha...  28.9 us
    pallas_call x1, Pallas kernels, shards(): pl.pallas_call(image_kernel, name='image_terms', out_shape=jax.ShapeDtype...  13.1 us
    unnamed x29, local copies, waits for them, and re-layouts  2.73 us

profile of v5, /device:TPU:1, one launch (start us, length us, event | category | flops | bytes accessed | tf_op | source)
XLA Modules:
  0.0 103.8 jit_solution(2428766019497794505)
XLA Ops:
  0.0 0.0 copy-start.1
  0.0 0.0 copy-start
  0.0 0.0 copy-start.3
  0.0 0.0 copy-start.4
  0.0 1.1 %copy-done.4 = bf16[1,2,256,256]{3,2,1,0:T(8,128)(2,1)S(1)} copy-done((bf16[1,2,256,256]{3,2,1,0:T(8,128)(2,1)S(1)}, bf16[1,2,256,256]{3,2,1,0:T(8,128)(2,1)}, u32[]{:S(2)}) %copy-start.4) | copy-done | bytes 262168
  1.1 0.0 copy-start.5
  1.1 0.9 copy-done.5
  2.0 0.0 copy-start.6
  2.0 0.0 copy-start.7
  2.0 0.0 copy-start.8
  2.0 0.0 copy-start.10
  2.0 0.0 copy-start.11
  2.1 0.0 copy-start.12
  2.1 0.0 copy-start.13
  2.1 28.9 %gather_references.1 = bf16[4,8,144,256]{3,2,1,0:T(8,128)(2,1)S(1)} custom-call(bf16[2,256,256]{2,1,0:T(8,128)(2,1)S(1)} %bitcast.6, bf16[512,256]{1,0:T(8,128)(2,1)S(1)} %copy-done.5), custom_call_target="tpu_custom_call" | custom-call | tf_op jit(solution)/shard_map/gather_references/pallas_call | solution.py:687
  31.0 0.0 copy-done.1
  31.0 0.0 copy-done
  31.1 0.0 copy-done.3
  31.1 0.0 copy-done.6
  31.1 0.0 copy-done.7
  31.1 0.0 copy-done.8
  31.1 0.0 copy-done.10
  31.1 0.0 copy-done.11
  31.1 0.0 copy-done.12
  31.1 0.0 copy-done.13
  31.1 0.0 copy-start.2
  31.1 0.0 copy-start.9
  31.2 13.1 %image_terms.1 = bf16[32,144,256]{2,1,0:T(8,128)(2,1)S(1)} custom-call(s32[32]{0:T(128)S(1)} %bitcast.7, s32[32]{0:T(128)S(1)} %copy-done.12, s32[32]{0:T(128)S(1)} %copy-done.13, bf16[32,256,256]{2,1,0:T(8,128)(2,1)} %img_ref.1, bf16[32,144,256]{2,1,0:T(8,128)(2,1)S(1)} %bitcast.5, f32[16,128,128]{2,1,0:T(8,128)S(1)} %copy-done, ...), custom_call_target="tpu_custom_call" | custom-call | tf_op jit(solution)/shard_map/image_terms/pallas_call | solution.py:702
  44.3 0.0 copy-done.2
  44.3 0.0 copy-done.9
  44.3 58.8 %reduce_maps.1 = f32[1,128,256]{2,1,0:T(8,128)S(1)} custom-call(bf16[4,8,144,256]{3,2,1,0:T(8,128)(2,1)S(1)} %bitcast.4, f32[16,128,128]{2,1,0:T(8,128)S(1)} %copy-done, s32[64,128]{1,0:T(8,128)S(1)} %copy-done.9, bf16[768,256]{1,0:T(8,128)(2,1)S(1)} %copy-done.1, bf16[768,144]{1,0:T(8,128)(2,1)S(1)} %copy-done.2), custom_call_target="tpu_custom_call" | custom-call | tf_op jit(solution)/shard_map/reduce_maps/pallas_call | solution.py:728
  103.1 0.7 copy.17
Async XLA Ops:
  0.0 31.0 %copy-start.1 = (bf16[768,256]{1,0:T(8,128)(2,1)S(1)}, bf16[768,256]{1,0:T(8,128)(2,1)}, u32[]{:S(2)}) copy-start(bf16[768,256]{1,0:T(8,128)(2,1)} %constant.24.clone.expand_ref.expand_any) | copy-start | bytes 1179652
  0.0 31.0 %copy-start = (f32[16,128,128]{2,1,0:T(8,128)S(1)}, f32[16,128,128]{2,1,0:T(8,128)}, u32[]{:S(2)}) copy-start(f32[16,128,128]{2,1,0:T(8,128)} %constant.23.clone.ctf_ref) | copy-start | bytes 3145732
  0.0 31.0 %copy-start.3 = (bf16[256,512]{1,0:T(8,128)(2,1)S(1)}, bf16[256,512]{1,0:T(8,128)(2,1)}, u32[]{:S(2)}) copy-start(bf16[256,512]{1,0:T(8,128)(2,1)} %constant.21.clone.widen_ref) | copy-start | bytes 786436
  0.0 1.1 %copy-start.4 = (bf16[1,2,256,256]{3,2,1,0:T(8,128)(2,1)S(1)}, bf16[1,2,256,256]{3,2,1,0:T(8,128)(2,1)}, u32[]{:S(2)}) copy-start(bf16[1,2,256,256]{3,2,1,0:T(8,128)(2,1)} %param.16) | copy-start | bytes 786436
  1.1 0.9 copy-start.5
  2.0 29.0 %copy-start.6 = (bf16[256,256]{1,0:T(8,128)(2,1)S(1)}, bf16[256,256]{1,0:T(8,128)(2,1)}, u32[]{:S(2)}) copy-start(bf16[256,256]{1,0:T(8,128)(2,1)} %constant.22.clone.combine_ref) | copy-start | bytes 393220
  2.0 29.0 %copy-start.7 = (bf16[256,256]{1,0:T(8,128)(2,1)S(1)}, bf16[256,256]{1,0:T(8,128)(2,1)}, u32[]{:S(2)}) copy-start(bf16[256,256]{1,0:T(8,128)(2,1)} %constant.19.clone.cst_ref) | copy-start | bytes 393220
  2.0 29.0 %copy-start.8 = (bf16[256,256]{1,0:T(8,128)(2,1)S(1)}, bf16[256,256]{1,0:T(8,128)(2,1)}, u32[]{:S(2)}) copy-start(bf16[256,256]{1,0:T(8,128)(2,1)} %constant.18.clone.cs_ref) | copy-start | bytes 393220
  2.0 29.1 %copy-start.10 = (bf16[64,64]{1,0:T(8,128)(2,1)S(1)}, bf16[64,64]{1,0:T(8,128)(2,1)}, u32[]{:S(2)}) copy-start(bf16[64,64]{1,0:T(8,128)(2,1)} %constant.25.clone.turn_ref) | copy-start | bytes 24580
  2.0 29.1 %copy-start.11 = (s32[32,1]{0,1:T(1,128)S(1)}, s32[32,1]{0,1:T(1,128)}, u32[]{:S(2)}) copy-start(s32[32,1]{0,1:T(1,128)} %param.17) | copy-start | bytes 388
  2.1 29.1 %copy-start.12 = (s32[32]{0:T(128)S(1)}, s32[32]{0:T(128)}, u32[]{:S(2)}) copy-start(s32[32]{0:T(128)} %class_ref.1) | copy-start | bytes 388
  2.1 29.1 %copy-start.13 = (s32[32]{0:T(128)S(1)}, s32[32]{0:T(128)}, u32[]{:S(2)}) copy-start(s32[32]{0:T(128)} %bin_ref.1) | copy-start | bytes 388
  31.1 13.2 %copy-start.2 = (bf16[768,144]{1,0:T(8,128)(2,1)S(1)}, bf16[768,144]{1,0:T(8,128)(2,1)}, u32[]{:S(2)}) copy-start(bf16[768,144]{1,0:T(8,128)(2,1)} %constant.26.clone.left_any) | copy-start | bytes 663556
  31.1 13.2 %copy-start.9 = (s32[64,128]{1,0:T(8,128)S(1)}, s32[64,128]{1,0:T(8,128)}, u32[]{:S(2)}) copy-start(s32[64,128]{1,0:T(8,128)} %cells_ref.1) | copy-start | bytes 98308
